TPU v7x, 32 devices: a whole 2x2x4 slice. The times are simulated.
32 devices in a mesh: groups: 2 (over y), tp: 4 (over z), sp: 4 (over x, core).
Axes of the slice: x: 2, y: 2, z: 4, core: 2. Of those that a mesh axis runs over, the one named last changes fastest.
Arguments:
- hidden_cont: bfloat16 [512, 5120], P(('groups', 'sp')), parts along dimension 0, may hold values from -6 to 6
- hidden_prompt: bfloat16 [1024, 5120], P(('groups', 'sp')), parts along dimension 0, may hold values from -6 to 6
- norm_gain: float32 [5120], replicated, may hold values from 0.1 to 1.9
- query_weight: bfloat16 [5120, 4096], P('sp', 'tp'), may hold values from -0.078125 to 0.078125
- keyval_weight: bfloat16 [5120, 1024], P('sp'), may hold values from -0.078125 to 0.078125
- out_weight: bfloat16 [4096, 5120], P('tp', 'sp'), may hold values from -0.125 to 0.125
- query_gain: float32 [128], replicated, may hold values from 0.5 to 5
- key_gain: float32 [128], replicated, may hold values from 0.5 to 5
- sample_lengths: int32 [16], P('groups'), parts along dimension 0, may hold values from 1 to 64, 256 in all
Outputs:
- mixed: bfloat16 [512, 5120], P(('groups', 'sp'), 'tp'), parts along dimension 0
There are 2 independent parts, one for each index of `groups`. A program takes and returns all parts, laid end to end along the dimension named above; an argument that names none is the same for every part. Nothing has to cross between parts.
Inputs may be any that keep to these rules, and one draw needn't show every extreme that they name: `sample_lengths`: the lengths sum to 256 and the longest has exactly 64 tokens.
All inputs are finite; a program needn't handle non-finite values.
Results may differ from a plain program's by a relative error of at most 0.012.
The roundings to bfloat16 on the way count: a program that leaves them out, or rounds other values in their place, can miss the bound.
Values may be sent and summed in bfloat16 or wider, within the bound.
No kernel may reach another device: no remote copies, remote signals or barrier semaphores. Data moves between devices by JAX's collectives and lax.ppermute only.
A program may use at most 128 MiB of HBM per device.

v0:
```python
import math

import jax
import jax.numpy as jnp
from jax import lax
from jax.sharding import PartitionSpec as P

QH = 32
KVH = 4


def rms_rows(values, gain):
    return values * lax.rsqrt(jnp.mean(values * values, axis=-1, keepdims=True) + 1e-06) * gain


def rotate(values, positions):
    half = values.shape[-1] // 2
    frequency = jnp.exp(
        jnp.arange(half, dtype=jnp.float32) * (-2.0 * math.log(1000000.0) / values.shape[-1])
    )
    angles = positions.astype(jnp.float32)[:, None] * frequency[None, :]
    shape = (positions.shape[0],) + (1,) * (values.ndim - 2) + (half,)
    cosine = jnp.cos(angles).reshape(shape)
    sine = jnp.sin(angles).reshape(shape)
    first = values[..., :half]
    second = values[..., half:]
    return jnp.concatenate(
        [first * cosine - second * sine, second * cosine + first * sine], axis=-1
    )


def segments(lengths, index):
    ends = jnp.cumsum(lengths, dtype=jnp.int32)
    segment = jnp.sum((index[:, None] >= ends[None, :]).astype(jnp.int32), axis=1, dtype=jnp.int32)
    member = segment[:, None] == jnp.arange(lengths.shape[0], dtype=jnp.int32)[None, :]
    start = jnp.sum(jnp.where(member, (ends - lengths)[None, :], 0), axis=1, dtype=jnp.int32)
    return (segment, start)


def attend(query, keys, values, allowed, scale):
    scores = (
        lax.dot_general(query, keys, (((1,), (1,)), ((), ())), preferred_element_type=jnp.float32)
        * scale
    )
    scores = jnp.where(allowed, scores, -1e30)
    peak = jnp.max(scores, axis=1, keepdims=True)
    raised = jnp.exp(scores - peak)
    weights = (raised / jnp.sum(raised, axis=1, keepdims=True)).astype(jnp.bfloat16)
    return jnp.dot(weights, values, preferred_element_type=jnp.float32).astype(jnp.bfloat16)


def add_rows(left, piece):
    return jnp.dot(left, piece, preferred_element_type=jnp.float32)


def on_device(
    hidden_cont,
    hidden_prompt,
    norm_gain,
    query_weight,
    keyval_weight,
    out_weight,
    query_gain,
    key_gain,
    sample_lengths,
):
    head_size = query_gain.shape[0]
    heads_here = query_weight.shape[1] // head_size
    cont_rows = hidden_cont.shape[0]
    prompt_rows = hidden_prompt.shape[0]
    tp_index = lax.axis_index("tp")
    sp_index = lax.axis_index("sp")
    sp_count = lax.axis_size("sp")
    cont_total = cont_rows * sp_count
    prompt_total = prompt_rows * sp_count
    key_head = tp_index * heads_here // (QH // KVH)
    scale = 1.0 / math.sqrt(head_size)
    normed_cont = rms_rows(hidden_cont.astype(jnp.float32), norm_gain).astype(jnp.bfloat16)
    normed_prompt = rms_rows(hidden_prompt.astype(jnp.float32), norm_gain).astype(jnp.bfloat16)
    normed_all = jnp.concatenate([normed_prompt, normed_cont], axis=0)
    kv_weight = lax.dynamic_slice_in_dim(keyval_weight, key_head * 2 * head_size, 2 * head_size, 1)
    query = add_rows(normed_cont, lax.all_gather(query_weight, "sp", axis=0, tiled=True))
    keyval = add_rows(normed_all, lax.all_gather(kv_weight, "sp", axis=0, tiled=True))
    cont_index = sp_index * cont_rows + jnp.arange(cont_rows, dtype=jnp.int32)
    row_segment, row_start = segments(sample_lengths, cont_index)
    cont_pos = prompt_total + cont_index - row_start
    prompt_pos = sp_index * prompt_rows + jnp.arange(prompt_rows, dtype=jnp.int32)
    positions = jnp.concatenate([prompt_pos, cont_pos])
    keys = rotate(rms_rows(keyval[:, :head_size], key_gain), positions).astype(jnp.bfloat16)
    values = keyval[:, head_size:].astype(jnp.bfloat16)
    local_pairs = jnp.concatenate([keys, values], axis=1)
    prompt_pairs, cont_pairs = (
        lax.all_gather(local_pairs[:prompt_rows], "sp", axis=0, tiled=True),
        lax.all_gather(local_pairs[prompt_rows:], "sp", axis=0, tiled=True),
    )
    all_keys = jnp.concatenate([prompt_pairs[:, :head_size], cont_pairs[:, :head_size]], axis=0)
    all_values = jnp.concatenate([prompt_pairs[:, head_size:], cont_pairs[:, head_size:]], axis=0)
    query = query.reshape(cont_rows, heads_here, head_size)
    query = rotate(rms_rows(query, query_gain), cont_pos).astype(jnp.bfloat16)
    total_rows = cont_rows * heads_here
    query = query.reshape(total_rows, head_size)
    key_index = jnp.arange(cont_total, dtype=jnp.int32)
    key_segment, key_start = segments(sample_lengths, key_index)
    row_index = jnp.repeat(cont_index, heads_here)
    row_owner = jnp.repeat(row_segment, heads_here)
    block_rows = 512 if total_rows % 512 == 0 else total_rows
    block_count = total_rows // block_rows

    def one_block(block):
        own_part = (key_segment[None, :] == row_owner[:, None]) & (
            key_index[None, :] <= row_index[:, None]
        )
        allowed = jnp.concatenate(
            [jnp.ones((block_rows, prompt_total), dtype=jnp.bool_), own_part], axis=1
        )
        return attend(query, all_keys, all_values, allowed, scale)

    heads = lax.map(one_block, jnp.arange(block_count, dtype=jnp.int32))
    heads = heads.reshape(cont_rows, heads_here * head_size)
    partial_out = jnp.dot(
        heads,
        lax.all_gather(out_weight, "sp", axis=1, tiled=True),
        preferred_element_type=jnp.float32,
    )
    summed = lax.psum_scatter(
        partial_out.astype(jnp.bfloat16), "tp", scatter_dimension=1, tiled=True
    ).astype(jnp.float32)
    out_width = summed.shape[1]
    residual = lax.dynamic_slice_in_dim(hidden_cont, tp_index * out_width, out_width, 1).astype(
        jnp.float32
    )
    return (summed + residual).astype(jnp.bfloat16)


def solution(mesh):
    placed = (
        P(("groups", "sp"), None),
        P(("groups", "sp"), None),
        P(),
        P("sp", "tp"),
        P("sp", None),
        P("tp", "sp"),
        P(),
        P(),
        P("groups"),
    )
    return jax.shard_map(
        on_device, mesh=mesh, in_specs=placed, out_specs=P(("groups", "sp"), "tp"), check_vma=False
    )
```

profile of v0, /device:TPU:1, one launch (start us, length us, event | category | flops | bytes accessed | tf_op | source)
XLA Modules:
  0.0 216.2 jit_solution(8634546538117229407)
XLA Ops:
  6.5 1.7 copy-done
  8.3 1.0 constant_dynamic-slice_fusion
  9.3 0.7 all-gather.4.cloned.1.call-update
  10.1 0.7 all-gather.8.cloned.1.call-update
  12.2 1.8 fusion
  13.9 0.8 multiply_cosine_fusion.1
  15.2 1.4 fusion.2
  16.7 20.8 %all-gather.6.cloned.1.call-done = bf16[5120,256]{1,0:T(8,128)(2,1)} async-done(((bf16[1280,256]{1,0:T(8,128)(2,1)}), bf16[5120,256]{1,0:T(8,128)(2,1)}) %all-gather.6.cloned.1.call-update) | async-done | bytes 2621456 | tf_op jit(solution)/shard_map/all_gather | solution.py:83
  37.5 2.8 %fusion.3 = f32[192,256]{1,0:T(8,128)S(1)} fusion(bf16[5120,256]{1,0:T(8,128)(2,1)} %all-gather.6.cloned.1.call-done, bf16[64,5120]{1,0:T(8,128)(2,1)S(1)} %fusion.10, bf16[128,5120]{1,0:T(8,128)(2,1)} %fusion.2), kind=kOutput, calls=%fused_computation.6 | convolution fusion | flops 507248640 | bytes 4784128 | tf_op jit(solution)/shard_map/dot_general | solution.py:53
  40.6 0.5 fusion.28
  41.2 5.5 %all_gather.18 = bf16[256,256]{1,0:T(8,128)(2,1)S(1)} all-gather(bf16[64,256]{1,0:T(8,128)(2,1)S(1)} %pad_maximum_fusion.1), channel_id=1, replica_groups=mesh['groups'=2,'tp'=4,'sp'=4] {'sp'}, dimensions={0}, use_global_device_ids=true | all-gather | bytes 163840 | tf_op jit(solution)/shard_map/all_gather | solution.py:94
  46.7 6.7 %all_gather.17 = bf16[512,256]{1,0:T(8,128)(2,1)S(1)} all-gather(bf16[128,256]{1,0:T(8,128)(2,1)S(1)} %slice.55), channel_id=1, replica_groups=mesh['groups'=2,'tp'=4,'sp'=4] {'sp'}, dimensions={0}, use_global_device_ids=true | all-gather | bytes 327680 | tf_op jit(solution)/shard_map/all_gather | solution.py:93
  53.5 0.6 fusion.36
  54.1 0.7 fusion.35
  54.8 54.9 %all-gather.4.cloned.1.call-done = bf16[5120,1024]{1,0:T(8,128)(2,1)} async-done(((bf16[1280,1024]{1,0:T(8,128)(2,1)}), bf16[5120,1024]{1,0:T(8,128)(2,1)}) %all-gather.4.cloned.1.call-update) | async-done | bytes 10485776 | tf_op jit(solution)/shard_map/all_gather | solution.py:82
  109.7 5.9 %convolution_bitcast_fusion = f32[8,8,8,128]{3,1,2,0:T(8,128)S(1)} fusion(bf16[64,5120]{1,0:T(8,128)(2,1)S(1)} %fusion.10, bf16[5120,1024]{1,0:T(8,128)(2,1)} %all-gather.4.cloned.1.call-done), kind=kOutput, calls=%fused_computation.19 | convolution fusion | flops 671088640 | bytes 11403264 | tf_op jit(solution)/shard_map/dot_general | solution.py:53
  116.2 0.9 fusion.22
  117.1 1.4 fusion.37
  118.5 0.4 fusion.7
  118.9 0.5 convolution_convert_fusion.1
  119.5 62.0 %all-gather.8.cloned.1.call-done = bf16[1024,5120]{1,0:T(8,128)(2,1)} async-done(((bf16[1024,1280]{1,0:T(8,128)(2,1)}), bf16[1024,5120]{1,0:T(8,128)(2,1)}) %all-gather.8.cloned.1.call-update) | async-done | bytes 10485776 | tf_op jit(solution)/shard_map/all_gather | solution.py:122
  181.5 6.8 %convolution_convert_fusion = bf16[64,5120]{1,0:T(8,128)(2,1)} fusion(bf16[64,1024]{1,0:T(8,128)(2,1)S(1)} %reshape.159, bf16[1024,5120]{1,0:T(8,128)(2,1)} %all-gather.8.cloned.1.call-done), kind=kOutput, calls=%fused_computation | convolution fusion | flops 671416320 | bytes 11272192 | tf_op jit(solution)/shard_map/dot_general | solution.py:120
  188.3 19.6 %reduce-scatter.2.cloned.1.call-done = bf16[64,1280]{1,0:T(8,128)(2,1)} async-done(((bf16[64,5120]{1,0:T(8,128)(2,1)}), bf16[64,1280]{1,0:T(8,128)(2,1)}) %reduce-scatter.2.cloned.1.call-update) | async-done | bytes 163856 | tf_op jit(solution)/shard_map/reduce_scatter | solution.py:125
  207.9 1.7 add_convert_fusion
  (58 shorter events, 2.8 us)
Async XLA Ops:
  6.5 1.7 copy-start
  6.5 30.9 %all-gather.6.cloned.1.call-start = ((), (), s32[]{:S(2)}) async-start(), calls=%async_computation.2 | async-start | bytes 3276800 | tf_op jit(solution)/shard_map/all_gather | solution.py:83
  9.3 100.4 %all-gather.4.cloned.1.call-start = ((), (), s32[]{:S(2)}) async-start(), calls=%async_computation.1 | async-start | bytes 13107200 | tf_op jit(solution)/shard_map/all_gather | solution.py:82
  10.0 0.8 copy-start.9
  10.0 1.9 copy-start.2
  10.1 171.5 %all-gather.8.cloned.1.call-start = ((), (), s32[]{:S(2)}) async-start(), calls=%async_computation.3 | async-start | bytes 13107200 | tf_op jit(solution)/shard_map/all_gather | solution.py:122
  10.8 4.2 %copy-start.5 = (f32[5120]{0:T(1024)S(1)}, f32[5120]{0:T(1024)}, u32[]{:S(2)}) copy-start(f32[5120]{0:T(1024)} %param.11) | copy-start | bytes 61444
  10.8 197.1 %reduce-scatter.2.cloned.1.call-start = ((), (), s32[]{:S(2)}) async-start(), calls=%async_computation.4 | async-start | bytes 819200 | tf_op jit(solution)/shard_map/reduce_scatter | solution.py:125
  11.6 3.4 %copy-start.3 = (bf16[64,5120]{1,0:T(8,128)(2,1)S(1)}, bf16[64,5120]{1,0:T(8,128)(2,1)}, u32[]{:S(2)}) copy-start(bf16[64,5120]{1,0:T(8,128)(2,1)} %param.9) | copy-start | bytes 1966084
  12.2 3.1 %copy-start.1 = (bf16[128,5120]{1,0:T(8,128)(2,1)S(1)}, bf16[128,5120]{1,0:T(8,128)(2,1)}, u32[]{:S(2)}) copy-start(bf16[128,5120]{1,0:T(8,128)(2,1)} %param.10) | copy-start | bytes 3932164
  16.7 23.8 %copy-start.7 = (f32[128]{0:T(128)S(1)}, f32[128]{0:T(128)}, u32[]{:S(2)}) copy-start(f32[128]{0:T(128)} %param.16) | copy-start | bytes 1540
  54.8 61.2 %copy-start.8 = (f32[128]{0:T(128)S(1)}, f32[128]{0:T(128)}, u32[]{:S(2)}) copy-start(f32[128]{0:T(128)} %param.15) | copy-start | bytes 1540
  115.6 1.5 copy-start.4
  117.1 1.8 copy-start.6
Sparse Core Ops, SparseCore 0:
  9.4 28.0 all-gather.5
  39.0 70.6 all-gather.3
  111.3 70.1 all-gather.7
  188.5 19.4 reduce-scatter.1
where the time goes:
time: 219 us; the launch traced here: 216 us
  waiting for transfers between devices  159 us (73%)
  matrix products  17.4 us (8%)
  between operations  13.4 us (6%)
  blocking collectives  12.2 us (6%)
  other arithmetic  9.49 us (4%)
  local copies, waits for them, and re-layouts  4.71 us (2%)
    all_gather x1, waiting for transfers between devices, on_device(): lax.all_gather(out_weight, 'sp', axis=1, tiled=True)  62 us
    all_gather x1, waiting for transfers between devices, on_device(): lax.all_gather(query_weight, 'sp', axis=0, tiled=True)  54.9 us
    all_gather x1, waiting for transfers between devices, on_device(): lax.all_gather(kv_weight, 'sp', axis=0, tiled=True)  20.8 us
    reduce_scatter x1, waiting for transfers between devices, on_device(): lax.psum_scatter(partial_out.astype(jnp.bfloat16), 'tp', scatter_dimensio...  19.6 us
    dot_general x2, matrix products, add_rows(): return jnp.dot(left, piece, preferred_element_type=jnp.float32)  8.72 us
    dot_general x1, matrix products, on_device(): jnp.dot(heads, lax.all_gather(out_weight, 'sp', axis=1, tiled=True), pref...  6.78 us
    all_gather x1, blocking collectives, on_device(): lax.all_gather(local_pairs[:prompt_rows], 'sp', axis=0, tiled=True)  6.72 us
    all_gather x1, blocking collectives, on_device(): lax.all_gather(local_pairs[prompt_rows:], 'sp', axis=0, tiled=True)  5.52 us
  transfers between devices with their start and end apart: 4, of which 4 were waited for; matrix products, arithmetic and copies ran while one was open for 9% of the time, Pallas kernels for 0%

commit v1 on v0

v1 whole, which is shorter than its diff:
```python
import math

import jax
import jax.numpy as jnp
from jax import lax
from jax.sharding import PartitionSpec as P

QH = 32
KVH = 4


def rms_rows(values, gain):
    return values * lax.rsqrt(jnp.mean(values * values, axis=-1, keepdims=True) + 1e-06) * gain


def rotate(values, positions):
    half = values.shape[-1] // 2
    frequency = jnp.exp(
        jnp.arange(half, dtype=jnp.float32) * (-2.0 * math.log(1000000.0) / values.shape[-1])
    )
    angles = positions.astype(jnp.float32)[:, None] * frequency[None, :]
    shape = (positions.shape[0],) + (1,) * (values.ndim - 2) + (half,)
    cosine = jnp.cos(angles).reshape(shape)
    sine = jnp.sin(angles).reshape(shape)
    first = values[..., :half]
    second = values[..., half:]
    return jnp.concatenate(
        [first * cosine - second * sine, second * cosine + first * sine], axis=-1
    )


def segments(lengths, index):
    ends = jnp.cumsum(lengths, dtype=jnp.int32)
    segment = jnp.sum((index[:, None] >= ends[None, :]).astype(jnp.int32), axis=1, dtype=jnp.int32)
    member = segment[:, None] == jnp.arange(lengths.shape[0], dtype=jnp.int32)[None, :]
    start = jnp.sum(jnp.where(member, (ends - lengths)[None, :], 0), axis=1, dtype=jnp.int32)
    return (segment, start)


def attend(query, keys, values, allowed, scale):
    scores = (
        lax.dot_general(query, keys, (((1,), (1,)), ((), ())), preferred_element_type=jnp.float32)
        * scale
    )
    scores = jnp.where(allowed, scores, -1e30)
    peak = jnp.max(scores, axis=1, keepdims=True)
    raised = jnp.exp(scores - peak)
    weights = (raised / jnp.sum(raised, axis=1, keepdims=True)).astype(jnp.bfloat16)
    return jnp.dot(weights, values, preferred_element_type=jnp.float32).astype(jnp.bfloat16)


def swap(array, axis, bits):
    return lax.ppermute(array, axis, [(i, i ^ bits) for i in range(lax.axis_size(axis))])


def swap_bits(count):
    bits = []
    bit = 1
    while bit < count:
        bits.append(bit)
        bit *= 2
    return bits


def gather_blocks(block, axis, count):
    held = {0: block}
    bits = swap_bits(count)
    for bit in bits[1:] + bits[:1]:
        held.update({d ^ bit: swap(held[d], axis, bit) for d in sorted(held)})
    return [held[d] for d in range(count)]


def sum_blocks(blocks, axis, count):
    held = dict(enumerate(blocks))
    for bit in swap_bits(count):
        sent = [d for d in sorted(held) if d & bit]
        got = {d ^ bit: swap(held[d], axis, bit) for d in sent}
        held = {d: held[d] + got[d] for d in got}
    return held[0]


def on_device(
    hidden_cont,
    hidden_prompt,
    norm_gain,
    query_weight,
    keyval_weight,
    out_weight,
    query_gain,
    key_gain,
    sample_lengths,
):
    head_size = query_gain.shape[0]
    heads_here = query_weight.shape[1] // head_size
    cont_rows = hidden_cont.shape[0]
    prompt_rows = hidden_prompt.shape[0]
    depth = query_weight.shape[0]
    tp_index = lax.axis_index("tp")
    sp_index = lax.axis_index("sp")
    sp_count = lax.axis_size("sp")
    tp_count = lax.axis_size("tp")
    prompt_total = prompt_rows * sp_count
    key_head = tp_index * heads_here // (QH // KVH)
    scale = 1.0 / math.sqrt(head_size)
    owners = [sp_index ^ d for d in range(sp_count)]

    def column_block(array, owner):
        return lax.dynamic_slice_in_dim(array, owner * depth, depth, 1)

    normed_cont = rms_rows(hidden_cont.astype(jnp.float32), norm_gain).astype(jnp.bfloat16)
    cont_columns = [column_block(normed_cont, owner) for owner in owners]
    kv_weight = lax.dynamic_slice_in_dim(keyval_weight, key_head * 2 * head_size, 2 * head_size, 1)
    cont_blocks = [cont_columns[0]] + [
        swap(cont_columns[d], "sp", d) for d in range(1, sp_count)
    ]
    kv_weights = gather_blocks(kv_weight, "sp", sp_count)

    query_part = jnp.dot(
        jnp.concatenate(cont_blocks, axis=0), query_weight, preferred_element_type=jnp.float32
    )
    query = sum_blocks(
        [query_part[d * cont_rows : (d + 1) * cont_rows] for d in range(sp_count)], "sp", sp_count
    )

    normed_prompt = rms_rows(hidden_prompt.astype(jnp.float32), norm_gain).astype(jnp.bfloat16)
    keyval = sum(
        jnp.dot(
            jnp.concatenate([column_block(normed_prompt, owner), columns], axis=0),
            weight,
            preferred_element_type=jnp.float32,
        )
        for owner, columns, weight in zip(owners, cont_columns, kv_weights)
    )
    cont_index = sp_index * cont_rows + jnp.arange(cont_rows, dtype=jnp.int32)
    row_segment, row_start = segments(sample_lengths, cont_index)
    cont_pos = prompt_total + cont_index - row_start
    prompt_pos = sp_index * prompt_rows + jnp.arange(prompt_rows, dtype=jnp.int32)
    positions = jnp.concatenate([prompt_pos, cont_pos])
    keys = rotate(rms_rows(keyval[:, :head_size], key_gain), positions).astype(jnp.bfloat16)
    values = keyval[:, head_size:].astype(jnp.bfloat16)
    pairs = gather_blocks(jnp.concatenate([keys, values], axis=1), "sp", sp_count)
    pairs = jnp.concatenate(pairs, axis=0)
    all_keys = pairs[:, :head_size]
    all_values = pairs[:, head_size:]

    query = query.reshape(cont_rows, heads_here, head_size)
    query = rotate(rms_rows(query, query_gain), cont_pos).astype(jnp.bfloat16)
    query = query.reshape(cont_rows * heads_here, head_size)
    own_rows = jnp.arange(cont_rows, dtype=jnp.int32)
    key_index = jnp.concatenate(
        [
            part
            for owner in owners
            for part in (
                jnp.full((prompt_rows,), -1, dtype=jnp.int32),
                owner * cont_rows + own_rows,
            )
        ]
    )
    key_segment, _ = segments(sample_lengths, key_index)
    allowed = (key_index[None, :] < 0) | (
        (key_segment[None, :] == row_segment[:, None])
        & (key_index[None, :] <= cont_index[:, None])
    )
    allowed = jnp.broadcast_to(
        allowed[:, None, :], (cont_rows, heads_here, allowed.shape[1])
    ).reshape(cont_rows * heads_here, allowed.shape[1])
    heads = attend(query, all_keys, all_values, allowed, scale)
    heads = heads.reshape(cont_rows, heads_here * head_size)

    all_heads = jnp.concatenate(gather_blocks(heads, "sp", sp_count), axis=0)
    partial_out = jnp.dot(
        all_heads, out_weight, preferred_element_type=jnp.float32
    ).astype(jnp.bfloat16)
    assert tp_count == sp_count
    summed = 0.0
    for d in range(sp_count):
        block = lax.dynamic_slice_in_dim(
            partial_out, (tp_index ^ d ^ sp_index) * cont_rows, cont_rows, 0
        )
        block = lax.ppermute(
            block,
            ("tp", "sp"),
            [
                (t * sp_count + s, s * sp_count + (t ^ d))
                for t in range(tp_count)
                for s in range(sp_count)
            ],
        )
        summed = summed + block.astype(jnp.float32)
    out_width = summed.shape[1]
    residual = lax.dynamic_slice_in_dim(hidden_cont, tp_index * out_width, out_width, 1).astype(
        jnp.float32
    )
    return (summed + residual).astype(jnp.bfloat16)


def solution(mesh):
    placed = (
        P(("groups", "sp"), None),
        P(("groups", "sp"), None),
        P(),
        P("sp", "tp"),
        P("sp", None),
        P("tp", "sp"),
        P(),
        P(),
        P("groups"),
    )
    return jax.shard_map(
        on_device, mesh=mesh, in_specs=placed, out_specs=P(("groups", "sp"), "tp"), check_vma=False
    )
```

time: 219 us -> 99.6 us (0.45)
  the two profiles are of different devices: /device:TPU:1 before, /device:TPU:25 now
where the time goes in v1:
time: 99.6 us; the launch traced here: 99.2 us
  waiting for transfers between devices  43 us (43%)
  starting transfers between devices  22.9 us (23%)
  matrix products  13.5 us (14%)
  other arithmetic  11.1 us (11%)
  local copies, waits for them, and re-layouts  8.28 us (8%)
    ppermute x4, waiting for transfers between devices, on_device(): lax.ppermute(block, ('tp', 'sp'), [(t * sp_count + s, s * sp_count + (t ^...  24.8 us
    ppermute x15, waiting for transfers between devices, swap(): lax.ppermute(array, axis, [(i, i ^ bits) for i in range(lax.axis_size(axi...  18.2 us
    ppermute x15, starting transfers between devices, swap(): lax.ppermute(array, axis, [(i, i ^ bits) for i in range(lax.axis_size(axi...  15.3 us
    ppermute x4, starting transfers between devices, on_device(): lax.ppermute(block, ('tp', 'sp'), [(t * sp_count + s, s * sp_count + (t ^...  7.61 us
    dot_general x4, matrix products, on_device(): jnp.dot(jnp.concatenate([column_block(normed_prompt, owner), columns], ax...  6.66 us
    dynamic_slice x2, local copies, waits for them, and re-layouts, column_block(): return lax.dynamic_slice_in_dim(array, owner * depth, depth, 1)  3.04 us
    dot_general x1, matrix products, on_device(): jnp.dot(jnp.concatenate(cont_blocks, axis=0), query_weight, preferred_ele...  2.96 us
    reduce_sum x4, other arithmetic, rms_rows(): jnp.mean(values * values, axis=-1, keepdims=True) + 1e-06  2.85 us
  transfers between devices with their start and end apart: 19, of which 9 were waited for; matrix products, arithmetic and copies ran while one was open for 20% of the time, Pallas kernels for 0%

profile of v1, /device:TPU:25, one launch (start us, length us, event | category | flops | bytes accessed | tf_op | source)
XLA Modules:
  0.0 99.2 jit_solution(12793284298751716986)
XLA Ops:
  0.0 1.7 %copy-done = bf16[1280,1024]{1,0:T(8,128)(2,1)S(1)} copy-done((bf16[1280,1024]{1,0:T(8,128)(2,1)S(1)}, bf16[1280,1024]{1,0:T(8,128)(2,1)}, u32[]{:S(2)}) %copy-start) | copy-done | bytes 2621464
  5.9 1.9 %constant_dynamic-slice_fusion.9 = (bf16[64,1280]{1,0:T(8,128)(2,1)S(1)}, bf16[64,1280]{1,0:T(8,128)(2,1)}, bf16[64,1280]{1,0:T(8,128)(2,1)}, bf16[64,1280]{1,0:T(8,128)(2,1)}) fusion(bf16[64,5120]{1,0:T(8,128)(2,1)} %fusion.6, s32[]{:T(128)S(6)} %select_n.50, s32[]{:T(128)S(6)} %select_n.49, s32[]{:T(128)S(6)} %select_n.48, s32[]{:T(128)S(6)} %select_n.47), kind=kLoop, calls=%fused_computation.95 | loop fusion | bytes 1310736 | tf_op jit(solution)/shard_map/dynamic_slice | solution.py:108
  10.4 1.7 %fusion = f32[128]{0:T(128)S(1)} fusion(bf16[128,5120]{1,0:T(8,128)(2,1)} %param.10), kind=kLoop, calls=%fused_computation.2 | loop fusion | flops 1965952 | bytes 1311232 | tf_op jit(solution)/shard_map/reduce_sum | solution.py:13
  15.4 8.6 %collective-permute-done.2 = bf16[64,1280]{1,0:T(8,128)(2,1)} collective-permute-done((bf16[64,1280]{1,0:T(8,128)(2,1)S(1)}, bf16[64,1280]{1,0:T(8,128)(2,1)}, u32[]{:S(2)}, u32[]{:S(2)}) %collective-permute-start.2) | collective-permute-done | bytes 163872 | tf_op jit(solution)/shard_map/ppermute | solution.py:53
  24.0 3.0 %collective-permute-done.1 = bf16[64,1280]{1,0:T(8,128)(2,1)} collective-permute-done((bf16[64,1280]{1,0:T(8,128)(2,1)}, bf16[64,1280]{1,0:T(8,128)(2,1)}, u32[]{:S(2)}, u32[]{:S(2)}) %collective-permute-start.1) | collective-permute-done | bytes 163872 | tf_op jit(solution)/shard_map/ppermute | solution.py:53
  27.1 3.0 %fusion.7 = f32[256,1024]{1,0:T(8,128)S(1)} fusion(bf16[1280,1024]{1,0:T(8,128)(2,1)} %param.12, bf16[64,1280]{1,0:T(8,128)(2,1)} %collective-permute-done.2, bf16[64,1280]{1,0:T(8,128)(2,1)} %collective-permute-done.1, bf16[64,1280]{1,0:T(8,128)(2,1)} %collective-permute-done, bf16[64,1280]{1,0:T(8,128)(2,1)} %get-tuple-element.20), kind=kOutput, calls=%fused_computation.19 | convolution fusion | flops 673710080 | bytes 4325376 | tf_op jit(solution)/shard_map/dot_general | solution.py:118
  31.0 1.4 %fusion.22 = f32[192,256]{1,0:T(8,128)S(1)} fusion(bf16[1280,256]{1,0:T(8,128)(2,1)} %constant_dynamic-slice_fusion.7, bf16[64,1280]{1,0:T(8,128)(2,1)S(1)} %copy-done.8, bf16[128,1280]{1,0:T(8,128)(2,1)S(1)} %copy-done.5), kind=kOutput, calls=%fused_computation.34 | convolution fusion | flops 126812160 | bytes 1343488 | tf_op jit(solution)/shard_map/dot_general | solution.py:127
  32.5 1.3 %collective-permute-start.5 = (f32[64,1024]{1,0:T(8,128)S(1)}, f32[64,1024]{1,0:T(8,128)S(1)}, u32[]{:S(2)}, u32[]{:S(2)}) collective-permute-start(f32[64,1024]{1,0:T(8,128)S(1)} %slice_add_fusion), channel_id=1, source_target_pairs={{0,2},{1,3},{2,0},{3,1},{4,6},{5,7},{6,4},{7,5},{8,10},{9,11},{10,... | collective-permute-start | bytes 786440 | tf_op jit(solution)/shard_map/ppermute | solution.py:53
  34.5 1.5 %convolution_add_fusion.2 = f32[192,256]{1,0:T(8,128)S(1)} fusion(f32[192,256]{1,0:T(8,128)S(1)} %fusion.22, bf16[1280,256]{1,0:T(8,128)(2,1)} %collective-permute-done.6, bf16[64,1280]{1,0:T(8,128)(2,1)} %get-tuple-element.19, bf16[128,1280]{1,0:T(8,128)(2,1)S(1)} %copy-done.4), kind=kOutput, calls=%fused_computation.18 | convolution fusion | flops 126861312 | bytes 1540096 | tf_op jit(solution)/shard_map/dot_general | solution.py:127
  36.0 2.2 %convolution_add_fusion.1 = f32[192,256]{1,0:T(8,128)} fusion(f32[192,256]{1,0:T(8,128)S(1)} %convolution_add_fusion.2, bf16[1280,256]{1,0:T(8,128)(2,1)} %collective-permute-done.7, bf16[64,1280]{1,0:T(8,128)(2,1)} %get-tuple-element.18, bf16[128,1280]{1,0:T(8,128)(2,1)S(1)} %copy-done.3), kind=kOutput, calls=%fused_computation.17 | convolution fusion | flops 126861312 | bytes 1540096 | tf_op jit(solution)/shard_map/dot_general | solution.py:127
  38.2 1.7 %collective-permute-done.5 = f32[64,1024]{1,0:T(8,128)S(1)} collective-permute-done((f32[64,1024]{1,0:T(8,128)S(1)}, f32[64,1024]{1,0:T(8,128)S(1)}, u32[]{:S(2)}, u32[]{:S(2)}) %collective-permute-start.5) | collective-permute-done | bytes 262176 | tf_op jit(solution)/shard_map/ppermute | solution.py:53
  42.4 1.6 %convolution_add_fusion = f32[192,256]{1,0:T(8,128)S(1)} fusion(f32[192,256]{1,0:T(8,128)} %convolution_add_fusion.1, bf16[1280,256]{1,0:T(8,128)(2,1)} %collective-permute-done.8, bf16[64,1280]{1,0:T(8,128)(2,1)} %copy-done.7, bf16[128,1280]{1,0:T(8,128)(2,1)} %get-tuple-element.7), kind=kOutput, calls=%fused_computation.16 | convolution fusion | flops 126861312 | bytes 1540096 | tf_op jit(solution)/shard_map/dot_general | solution.py:127
  45.5 1.3 %collective-permute-start.10 = (bf16[192,256]{1,0:T(8,128)(2,1)S(1)}, bf16[192,256]{1,0:T(8,128)(2,1)S(1)}, u32[]{:S(2)}, u32[]{:S(2)}) collective-permute-start(bf16[192,256]{1,0:T(8,128)(2,1)S(1)} %pad_maximum_fusion.1), channel_id=1, source_target_pairs={{0,2},{1,3},{2,0},{3,1},{4,6},{5,7},{6,4},{7,5},{8,10},{9,11},{10,... | collective-permute-start | bytes 294920 | tf_op jit(solution)/shard_map/ppermute | solution.py:53
  47.6 1.7 %collective-permute-start.9 = (bf16[192,256]{1,0:T(8,128)(2,1)S(1)}, bf16[192,256]{1,0:T(8,128)(2,1)S(1)}, u32[]{:S(2)}, u32[]{:S(2)}) collective-permute-start(bf16[192,256]{1,0:T(8,128)(2,1)S(1)} %pad_maximum_fusion.1), channel_id=1, source_target_pairs={{0,1},{1,0},{2,3},{3,2},{4,5},{5,4},{6,7},{7,6},{8,9},{9,8},{10,11... | collective-permute-start | bytes 294920 | tf_op jit(solution)/shard_map/ppermute | solution.py:53
  49.2 2.3 %collective-permute-start.11 = (bf16[192,256]{1,0:T(8,128)(2,1)S(1)}, bf16[192,256]{1,0:T(8,128)(2,1)S(1)}, u32[]{:S(2)}, u32[]{:S(2)}) collective-permute-start(bf16[192,256]{1,0:T(8,128)(2,1)S(1)} %collective-permute-done.10), channel_id=1, source_target_pairs={{0,1},{1,0},{2,3},{3,2},{4,5},{5,4},{6,7},{7,6},{8,9},{9,8},{10,11... | collective-permute-start | bytes 294920 | tf_op jit(solution)/shard_map/ppermute | solution.py:53
  54.2 1.3 %collective-permute-start.13 = (bf16[64,1024]{1,0:T(8,128)(2,1)S(1)}, bf16[64,1024]{1,0:T(8,128)(2,1)S(1)}, u32[]{:S(2)}, u32[]{:S(2)}) collective-permute-start(bf16[64,1024]{1,0:T(8,128)(2,1)S(1)} %reshape.260), channel_id=1, source_target_pairs={{0,2},{1,3},{2,0},{3,1},{4,6},{5,7},{6,4},{7,5},{8,10},{9,11},{10,... | collective-permute-start | bytes 393224 | tf_op jit(solution)/shard_map/ppermute | solution.py:53
  56.1 2.9 %collective-permute-done.13 = bf16[64,1024]{1,0:T(8,128)(2,1)S(1)} collective-permute-done((bf16[64,1024]{1,0:T(8,128)(2,1)S(1)}, bf16[64,1024]{1,0:T(8,128)(2,1)S(1)}, u32[]{:S(2)}, u32[]{:S(2)}) %collective-permute-start.13) | collective-permute-done | bytes 131104 | tf_op jit(solution)/shard_map/ppermute | solution.py:53
  61.3 2.7 %convolution_convert_fusion = bf16[256,1280]{1,0:T(8,128)(2,1)S(1)} fusion(bf16[1024,1280]{1,0:T(8,128)(2,1)} %param.14, bf16[64,1024]{1,0:T(8,128)(2,1)} %collective-permute-done.14, bf16[64,1024]{1,0:T(8,128)(2,1)S(1)} %collective-permute-done.13, bf16[64,1024]{1,0:T(8,128)(2,1)} %collective-permute-done.12, bf16[64,1024]{1,0:T(8,128)(2,1)S(1)} %reshape.260), kind=kOutput, calls=%fused_computation.5 | convolution fusion | flops 673513472 | bytes 3801088 | tf_op jit(solution)/shard_map/dot_general | solution.py:172
  66.3 2.3 %collective-permute-start.16 = (bf16[64,1280]{1,0:T(8,128)(2,1)}, bf16[64,1280]{1,0:T(8,128)(2,1)}, u32[]{:S(2)}, u32[]{:S(2)}) collective-permute-start(bf16[64,1280]{1,0:T(8,128)(2,1)} %get-tuple-element.16), channel_id=1, source_target_pairs={{0,1},{1,5},{2,9},{3,13},{4,0},{5,4},{6,8},{7,12},{8,3},{9,7},{10,... | collective-permute-start | bytes 491528 | tf_op jit(solution)/shard_map/ppermute | solution.py:181
  68.6 3.8 %collective-permute-start.15 = (bf16[64,1280]{1,0:T(8,128)(2,1)S(1)}, bf16[64,1280]{1,0:T(8,128)(2,1)}, u32[]{:S(2)}, u32[]{:S(2)}) collective-permute-start(bf16[64,1280]{1,0:T(8,128)(2,1)S(1)} %get-tuple-element.13), channel_id=1, source_target_pairs={{0,0},{1,4},{2,8},{3,12},{4,1},{5,5},{6,9},{7,13},{8,2},{9,6},{10,... | collective-permute-start | bytes 491528 | tf_op jit(solution)/shard_map/ppermute | solution.py:181
  72.4 2.4 %collective-permute-done.17 = bf16[64,1280]{1,0:T(8,128)(2,1)} collective-permute-done((bf16[64,1280]{1,0:T(8,128)(2,1)}, bf16[64,1280]{1,0:T(8,128)(2,1)}, u32[]{:S(2)}, u32[]{:S(2)}) %collective-permute-start.17) | collective-permute-done | bytes 163872 | tf_op jit(solution)/shard_map/ppermute | solution.py:181
  74.8 6.0 %collective-permute-done.16 = bf16[64,1280]{1,0:T(8,128)(2,1)} collective-permute-done((bf16[64,1280]{1,0:T(8,128)(2,1)}, bf16[64,1280]{1,0:T(8,128)(2,1)}, u32[]{:S(2)}, u32[]{:S(2)}) %collective-permute-start.16) | collective-permute-done | bytes 163872 | tf_op jit(solution)/shard_map/ppermute | solution.py:181
  80.8 16.4 %collective-permute-done.15 = bf16[64,1280]{1,0:T(8,128)(2,1)} collective-permute-done((bf16[64,1280]{1,0:T(8,128)(2,1)S(1)}, bf16[64,1280]{1,0:T(8,128)(2,1)}, u32[]{:S(2)}, u32[]{:S(2)}) %collective-permute-start.15) | collective-permute-done | bytes 163872 | tf_op jit(solution)/shard_map/ppermute | solution.py:181
  97.2 1.9 %add_convert_fusion = bf16[64,1280]{1,0:T(8,128)(2,1)} fusion(bf16[64,1280]{1,0:T(8,128)(2,1)} %collective-permute-done.18, bf16[64,1280]{1,0:T(8,128)(2,1)} %collective-permute-done.17, bf16[64,1280]{1,0:T(8,128)(2,1)} %collective-permute-done.16, bf16[64,1280]{1,0:T(8,128)(2,1)} %collective-permute-done.15, bf16[64,5120]{1,0:T(8,128)(2,1)S(1)} %copy-done.2, ...), kind=kLoop, calls=%fused_computation.48 | loop fusion | flops 819200 | bytes 983044 | tf_op jit(solution)/shard_map/convert_element_type | solution.py:195
  (97 shorter events, 24.2 us)
Async XLA Ops:
  0.0 4.8 %copy-start.12 = (f32[5120]{0:T(1024)S(1)}, f32[5120]{0:T(1024)}, u32[]{:S(2)}) copy-start(f32[5120]{0:T(1024)} %param.11) | copy-start | bytes 61444
  2.7 31.9 %collective-permute-start.6 = (bf16[1280,256]{1,0:T(8,128)(2,1)}, bf16[1280,256]{1,0:T(8,128)(2,1)}, u32[]{:S(2)}, u32[]{:S(2)}) collective-permute-start(bf16[1280,256]{1,0:T(8,128)(2,1)} %constant_dynamic-slice_fusion.7), channel_id=1, source_target_pairs={{0,1},{1,0},{2,3},{3,2},{4,5},{5,4},{6,7},{7,6},{8,9},{9,8},{10,11... | collective-permute-start | bytes 1966088 | tf_op jit(solution)/shard_map/ppermute | solution.py:53
  3.3 30.4 %collective-permute-start.7 = (bf16[1280,256]{1,0:T(8,128)(2,1)}, bf16[1280,256]{1,0:T(8,128)(2,1)}, u32[]{:S(2)}, u32[]{:S(2)}) collective-permute-start(bf16[1280,256]{1,0:T(8,128)(2,1)} %constant_dynamic-slice_fusion.7), channel_id=1, source_target_pairs={{0,2},{1,3},{2,0},{3,1},{4,6},{5,7},{6,4},{7,5},{8,10},{9,11},{10,... | collective-permute-start | bytes 1966088 | tf_op jit(solution)/shard_map/ppermute | solution.py:53
  4.6 5.4 %copy-start.13 = (s32[8]{0:T(128)S(1)}, s32[8]{0:T(128)}, u32[]{:S(2)}) copy-start(s32[8]{0:T(128)} %param.17) | copy-start | bytes 100
  7.8 16.2 %collective-permute-start.2 = (bf16[64,1280]{1,0:T(8,128)(2,1)S(1)}, bf16[64,1280]{1,0:T(8,128)(2,1)}, u32[]{:S(2)}, u32[]{:S(2)}) collective-permute-start(bf16[64,1280]{1,0:T(8,128)(2,1)S(1)} %get-tuple-element.17), channel_id=1, source_target_pairs={{0,3},{1,2},{2,1},{3,0},{4,7},{5,6},{6,5},{7,4},{8,11},{9,10},{10,... | collective-permute-start | bytes 491528 | tf_op jit(solution)/shard_map/ppermute | solution.py:53
  8.2 18.8 %collective-permute-start.1 = (bf16[64,1280]{1,0:T(8,128)(2,1)}, bf16[64,1280]{1,0:T(8,128)(2,1)}, u32[]{:S(2)}, u32[]{:S(2)}) collective-permute-start(bf16[64,1280]{1,0:T(8,128)(2,1)} %get-tuple-element.18), channel_id=1, source_target_pairs={{0,2},{1,3},{2,0},{3,1},{4,6},{5,7},{6,4},{7,5},{8,10},{9,11},{10,... | collective-permute-start | bytes 491528 | tf_op jit(solution)/shard_map/ppermute | solution.py:53
  9.4 17.6 %collective-permute-start = (bf16[64,1280]{1,0:T(8,128)(2,1)}, bf16[64,1280]{1,0:T(8,128)(2,1)}, u32[]{:S(2)}, u32[]{:S(2)}) collective-permute-start(bf16[64,1280]{1,0:T(8,128)(2,1)} %get-tuple-element.19), channel_id=1, source_target_pairs={{0,1},{1,0},{2,3},{3,2},{4,5},{5,4},{6,7},{7,6},{8,9},{9,8},{10,11... | collective-permute-start | bytes 491528 | tf_op jit(solution)/shard_map/ppermute | solution.py:53
  30.1 2.4 %collective-permute-start.4 = (f32[64,1024]{1,0:T(8,128)S(1)}, f32[64,1024]{1,0:T(8,128)S(1)}, u32[]{:S(2)}, u32[]{:S(2)}) collective-permute-start(f32[64,1024]{1,0:T(8,128)S(1)} %get-tuple-element.12), channel_id=1, source_target_pairs={{0,1},{1,0},{2,3},{3,2},{4,5},{5,4},{6,7},{7,6},{8,9},{9,8},{10,11... | collective-permute-start | bytes 786440 | tf_op jit(solution)/shard_map/ppermute | solution.py:53
  32.4 5.8 %collective-permute-start.3 = (f32[64,1024]{1,0:T(8,128)S(1)}, f32[64,1024]{1,0:T(8,128)S(1)}, u32[]{:S(2)}, u32[]{:S(2)}) collective-permute-start(f32[64,1024]{1,0:T(8,128)S(1)} %get-tuple-element.11), channel_id=1, source_target_pairs={{0,1},{1,0},{2,3},{3,2},{4,5},{5,4},{6,7},{7,6},{8,9},{9,8},{10,11... | collective-permute-start | bytes 786440 | tf_op jit(solution)/shard_map/ppermute | solution.py:53
  32.5 7.5 %collective-permute-start.5 = (f32[64,1024]{1,0:T(8,128)S(1)}, f32[64,1024]{1,0:T(8,128)S(1)}, u32[]{:S(2)}, u32[]{:S(2)}) collective-permute-start(f32[64,1024]{1,0:T(8,128)S(1)} %slice_add_fusion), channel_id=1, source_target_pairs={{0,2},{1,3},{2,0},{3,1},{4,6},{5,7},{6,4},{7,5},{8,10},{9,11},{10,... | collective-permute-start | bytes 786440 | tf_op jit(solution)/shard_map/ppermute | solution.py:53
  33.8 8.6 %collective-permute-start.8 = (bf16[1280,256]{1,0:T(8,128)(2,1)}, bf16[1280,256]{1,0:T(8,128)(2,1)}, u32[]{:S(2)}, u32[]{:S(2)}) collective-permute-start(bf16[1280,256]{1,0:T(8,128)(2,1)} %collective-permute-done.7), channel_id=1, source_target_pairs={{0,1},{1,0},{2,3},{3,2},{4,5},{5,4},{6,7},{7,6},{8,9},{9,8},{10,11... | collective-permute-start | bytes 1966088 | tf_op jit(solution)/shard_map/ppermute | solution.py:53
  42.4 9.1 %copy-start.10 = (f32[64,64]{1,0:T(8,128)S(1)}, f32[64,64]{1,0:T(8,128)}, u32[]{:S(2)}) copy-start(f32[64,64]{1,0:T(8,128)} %get-tuple-element.25) | copy-start | bytes 49156
  42.4 9.1 %copy-start.11 = (f32[64,64]{1,0:T(8,128)S(1)}, f32[64,64]{1,0:T(8,128)}, u32[]{:S(2)}) copy-start(f32[64,64]{1,0:T(8,128)} %get-tuple-element.26) | copy-start | bytes 49156
  44.0 8.5 %copy-start.6 = (pred[64,768]{1,0:T(8,128)(4,1)S(1)}, pred[64,768]{1,0:T(8,128)(4,1)}, u32[]{:S(2)}) copy-start(pred[64,768]{1,0:T(8,128)(4,1)} %and_or_fusion) | copy-start | bytes 147460
  45.5 3.8 %collective-permute-start.10 = (bf16[192,256]{1,0:T(8,128)(2,1)S(1)}, bf16[192,256]{1,0:T(8,128)(2,1)S(1)}, u32[]{:S(2)}, u32[]{:S(2)}) collective-permute-start(bf16[192,256]{1,0:T(8,128)(2,1)S(1)} %pad_maximum_fusion.1), channel_id=1, source_target_pairs={{0,2},{1,3},{2,0},{3,1},{4,6},{5,7},{6,4},{7,5},{8,10},{9,11},{10,... | collective-permute-start | bytes 294920 | tf_op jit(solution)/shard_map/ppermute | solution.py:53
  47.6 4.1 %collective-permute-start.9 = (bf16[192,256]{1,0:T(8,128)(2,1)S(1)}, bf16[192,256]{1,0:T(8,128)(2,1)S(1)}, u32[]{:S(2)}, u32[]{:S(2)}) collective-permute-start(bf16[192,256]{1,0:T(8,128)(2,1)S(1)} %pad_maximum_fusion.1), channel_id=1, source_target_pairs={{0,1},{1,0},{2,3},{3,2},{4,5},{5,4},{6,7},{7,6},{8,9},{9,8},{10,11... | collective-permute-start | bytes 294920 | tf_op jit(solution)/shard_map/ppermute | solution.py:53
  49.2 3.2 %collective-permute-start.11 = (bf16[192,256]{1,0:T(8,128)(2,1)S(1)}, bf16[192,256]{1,0:T(8,128)(2,1)S(1)}, u32[]{:S(2)}, u32[]{:S(2)}) collective-permute-start(bf16[192,256]{1,0:T(8,128)(2,1)S(1)} %collective-permute-done.10), channel_id=1, source_target_pairs={{0,1},{1,0},{2,3},{3,2},{4,5},{5,4},{6,7},{7,6},{8,9},{9,8},{10,11... | collective-permute-start | bytes 294920 | tf_op jit(solution)/shard_map/ppermute | solution.py:53
  54.2 4.8 %collective-permute-start.13 = (bf16[64,1024]{1,0:T(8,128)(2,1)S(1)}, bf16[64,1024]{1,0:T(8,128)(2,1)S(1)}, u32[]{:S(2)}, u32[]{:S(2)}) collective-permute-start(bf16[64,1024]{1,0:T(8,128)(2,1)S(1)} %reshape.260), channel_id=1, source_target_pairs={{0,2},{1,3},{2,0},{3,1},{4,6},{5,7},{6,4},{7,5},{8,10},{9,11},{10,... | collective-permute-start | bytes 393224 | tf_op jit(solution)/shard_map/ppermute | solution.py:53
  55.4 4.7 %collective-permute-start.12 = (bf16[64,1024]{1,0:T(8,128)(2,1)S(1)}, bf16[64,1024]{1,0:T(8,128)(2,1)}, u32[]{:S(2)}, u32[]{:S(2)}) collective-permute-start(bf16[64,1024]{1,0:T(8,128)(2,1)S(1)} %reshape.260), channel_id=1, source_target_pairs={{0,1},{1,0},{2,3},{3,2},{4,5},{5,4},{6,7},{7,6},{8,9},{9,8},{10,11... | collective-permute-start | bytes 393224 | tf_op jit(solution)/shard_map/ppermute | solution.py:53
  59.0 2.3 %collective-permute-start.14 = (bf16[64,1024]{1,0:T(8,128)(2,1)S(1)}, bf16[64,1024]{1,0:T(8,128)(2,1)}, u32[]{:S(2)}, u32[]{:S(2)}) collective-permute-start(bf16[64,1024]{1,0:T(8,128)(2,1)S(1)} %collective-permute-done.13), channel_id=1, source_target_pairs={{0,1},{1,0},{2,3},{3,2},{4,5},{5,4},{6,7},{7,6},{8,9},{9,8},{10,11... | collective-permute-start | bytes 393224 | tf_op jit(solution)/shard_map/ppermute | solution.py:53
  64.8 7.6 %collective-permute-start.18 = (bf16[64,1280]{1,0:T(8,128)(2,1)}, bf16[64,1280]{1,0:T(8,128)(2,1)}, u32[]{:S(2)}, u32[]{:S(2)}) collective-permute-start(bf16[64,1280]{1,0:T(8,128)(2,1)} %get-tuple-element.14), channel_id=1, source_target_pairs={{0,3},{1,7},{2,11},{3,15},{4,2},{5,6},{6,10},{7,14},{8,1},{9,5},{1... | collective-permute-start | bytes 491528 | tf_op jit(solution)/shard_map/ppermute | solution.py:181
  65.1 9.7 %collective-permute-start.17 = (bf16[64,1280]{1,0:T(8,128)(2,1)}, bf16[64,1280]{1,0:T(8,128)(2,1)}, u32[]{:S(2)}, u32[]{:S(2)}) collective-permute-start(bf16[64,1280]{1,0:T(8,128)(2,1)} %get-tuple-element.15), channel_id=1, source_target_pairs={{0,2},{1,6},{2,10},{3,14},{4,3},{5,7},{6,11},{7,15},{8,0},{9,4},{1... | collective-permute-start | bytes 491528 | tf_op jit(solution)/shard_map/ppermute | solution.py:181
  66.3 14.5 %collective-permute-start.16 = (bf16[64,1280]{1,0:T(8,128)(2,1)}, bf16[64,1280]{1,0:T(8,128)(2,1)}, u32[]{:S(2)}, u32[]{:S(2)}) collective-permute-start(bf16[64,1280]{1,0:T(8,128)(2,1)} %get-tuple-element.16), channel_id=1, source_target_pairs={{0,1},{1,5},{2,9},{3,13},{4,0},{5,4},{6,8},{7,12},{8,3},{9,7},{10,... | collective-permute-start | bytes 491528 | tf_op jit(solution)/shard_map/ppermute | solution.py:181
  68.6 28.6 %collective-permute-start.15 = (bf16[64,1280]{1,0:T(8,128)(2,1)S(1)}, bf16[64,1280]{1,0:T(8,128)(2,1)}, u32[]{:S(2)}, u32[]{:S(2)}) collective-permute-start(bf16[64,1280]{1,0:T(8,128)(2,1)S(1)} %get-tuple-element.13), channel_id=1, source_target_pairs={{0,0},{1,4},{2,8},{3,12},{4,1},{5,5},{6,9},{7,13},{8,2},{9,6},{10,... | collective-permute-start | bytes 491528 | tf_op jit(solution)/shard_map/ppermute | solution.py:181
  (9 other events, 33.3 us)

commit v2 on v0

v2 whole, which is shorter than its diff:
```python
import functools
import math

import jax
import jax.numpy as jnp
from jax import lax
from jax.experimental import pallas as pl
from jax.experimental.pallas import tpu as pltpu
from jax.sharding import PartitionSpec as P

QH = 32
KVH = 4
SP, TP, GROUP, HEAD = range(4)
BF16 = jnp.bfloat16
F32 = jnp.float32
ROOM = 24 * 1024 * 1024


def call(kernel, place, grid, in_specs, out_specs, out_shape, args, cost, scratch=()):
    flops, moved = cost
    return pl.pallas_call(
        kernel,
        out_shape=out_shape,
        grid_spec=pltpu.PrefetchScalarGridSpec(
            num_scalar_prefetch=1,
            grid=grid,
            in_specs=in_specs,
            out_specs=out_specs,
            scratch_shapes=scratch,
        ),
        compiler_params=pltpu.CompilerParams(vmem_limit_bytes=ROOM),
        cost_estimate=pl.CostEstimate(flops=flops, bytes_accessed=moved, transcendentals=0),
    )(place, *args)


def whole(array):
    zeros = (0,) * array.ndim
    return pl.BlockSpec(array.shape, lambda i, place: zeros)


def shape_of(shape, dtype):
    return jax.ShapeDtypeStruct(shape, dtype)


def rms_rows(values, gain):
    return values * lax.rsqrt(jnp.mean(values * values, axis=-1, keepdims=True) + 1e-06) * gain


def norm_kernel(place, hidden, gain, out):
    count, _, depth = out.shape
    normed = rms_rows(hidden[...].astype(F32), gain[...]).astype(BF16)
    for j in range(count):
        out[j] = normed[:, j * depth : (j + 1) * depth]


def norm_split(place, hidden, gain, count):
    rows, width = hidden.shape
    step = min(rows, 64)
    out = (count, rows, width // count)
    return call(
        norm_kernel,
        place,
        (rows // step,),
        [pl.BlockSpec((step, width), lambda i, place: (i, 0)), whole(gain)],
        pl.BlockSpec((count, step, width // count), lambda i, place: (0, i, 0)),
        shape_of(out, BF16),
        (hidden, gain),
        (4 * rows * width, 4 * rows * width),
    )


def pick_kernel(place, first, second, out_first, out_second):
    out_first[...] = first[...]
    out_second[...] = second[...]


def pick_columns(place, keyval_weight, head_size):
    depth = keyval_weight.shape[0]
    block = (depth, head_size)
    return call(
        pick_kernel,
        place,
        (1,),
        [
            pl.BlockSpec(block, lambda i, place: (0, 2 * place[HEAD] + place[GROUP])),
            pl.BlockSpec(block, lambda i, place: (0, 2 * place[HEAD] + 1 - place[GROUP])),
        ],
        [pl.BlockSpec(block, lambda i, place: (0, 0))] * 2,
        [shape_of(block, BF16)] * 2,
        (keyval_weight, keyval_weight),
        (0, 8 * depth * head_size),
    )


def query_kernel(count, place, rows, weight, *outs):
    block = rows.shape[1]
    left = jnp.concatenate([rows[place[SP] ^ d] for d in range(count)], axis=0)
    part = jnp.dot(left, weight[...], preferred_element_type=F32)
    for d in range(count):
        outs[d][...] = part[d * block : (d + 1) * block]


def query_parts(place, rows, weight):
    count, block, depth = rows.shape
    width = weight.shape[1]
    step = min(width, 256)
    return call(
        functools.partial(query_kernel, count),
        place,
        (width // step,),
        [whole(rows), pl.BlockSpec((depth, step), lambda i, place: (0, i))],
        [pl.BlockSpec((block, step), lambda i, place: (0, i))] * count,
        [shape_of((block, width), F32)] * count,
        (rows, weight),
        (2 * count * block * depth * width, 2 * depth * width),
    )


def turn(values, cosine, sine):
    return values * cosine + pltpu.roll(values, values.shape[-1] // 2, 1) * sine


def keyval_kernel(count, place, prompt, cont, cosine, sine, gain, *refs):
    weights, out = refs[:-1], refs[-1]
    prompt_rows = prompt.shape[1]
    size = gain.shape[1]
    sums = []
    for left in (prompt, cont):
        for half in range(2):
            total = 0.0
            for d in range(count):
                total = total + jnp.dot(
                    left[place[SP] ^ d],
                    weights[2 * d + half][...],
                    preferred_element_type=F32,
                )
            sums.append(total)
    swapped = place[GROUP] == 1
    for at, first, second in ((0, *sums[:2]), (prompt_rows, *sums[2:])):
        rows = slice(at, at + first.shape[0])
        key = jnp.where(swapped, second, first)
        value = jnp.where(swapped, first, second)
        key = turn(rms_rows(key, gain[...]), cosine[rows, :], sine[rows, :])
        out[rows, :size] = key.astype(BF16)
        out[rows, size:] = value.astype(BF16)


def keyval_rows(place, prompt, cont, cosine, sine, gain, weights):
    count, prompt_rows, depth = prompt.shape
    rows = prompt_rows + cont.shape[1]
    size = gain.shape[1]
    args = (prompt, cont, cosine, sine, gain, *weights)
    out = shape_of((rows, 2 * size), BF16)
    return call(
        functools.partial(keyval_kernel, count),
        place,
        (1,),
        [whole(a) for a in args],
        whole(out),
        out,
        args,
        (4 * rows * count * depth * size, 2 * count * depth * (rows + 2 * size)),
    )


def attend_kernel(count, prompt_rows, place, lengths, mine, other, cosine, sine, gain, *refs):
    pairs, out = refs[:-1], refs[-1]
    rows, width = mine.shape
    size = gain.shape[1]
    heads = width // size
    queries = []
    for h in range(heads):
        part = slice(h * size, (h + 1) * size)
        value = rms_rows(mine[:, part] + other[:, part], gain[...])
        queries.append(turn(value, cosine[...], sine[...]).astype(BF16))
    queries = jnp.concatenate(queries, axis=0)
    prompt = jnp.concatenate([pair[:prompt_rows] for pair in pairs], axis=0)
    cont = jnp.concatenate([pair[prompt_rows:] for pair in pairs], axis=0)
    scale = 1.0 / math.sqrt(size)
    by_rows = (((1,), (1,)), ((), ()))
    to_prompt = (
        lax.dot_general(queries, prompt[:, :size], by_rows, preferred_element_type=F32) * scale
    )
    to_cont = (
        lax.dot_general(queries, cont[:, :size], by_rows, preferred_element_type=F32) * scale
    )
    shape = (rows, cont.shape[0])
    own = place[SP] * rows + lax.broadcasted_iota(jnp.int32, shape, 0)
    at = lax.broadcasted_iota(jnp.int32, shape, 1)
    key = jnp.zeros(shape, jnp.int32)
    for d in range(count):
        inside = (at >= d * rows) & (at < (d + 1) * rows)
        key = jnp.where(inside, (place[SP] ^ d) * rows + at - d * rows, key)
    start = jnp.zeros(shape, jnp.int32)
    total = jnp.int32(0)
    for c in range(lengths.shape[0]):
        start = jnp.where(own >= total, total, start)
        total = total + lengths[c]
    allowed = jnp.where((key >= start) & (key <= own), 0.0, -1e30)
    to_cont = to_cont + jnp.concatenate([allowed] * heads, axis=0)
    peak = jnp.maximum(
        jnp.max(to_prompt, axis=1, keepdims=True), jnp.max(to_cont, axis=1, keepdims=True)
    )
    to_prompt = jnp.exp(to_prompt - peak)
    to_cont = jnp.exp(to_cont - peak)
    divisor = jnp.sum(to_prompt, axis=1, keepdims=True) + jnp.sum(to_cont, axis=1, keepdims=True)
    result = jnp.dot(
        (to_prompt / divisor).astype(BF16), prompt[:, size:], preferred_element_type=F32
    ) + jnp.dot((to_cont / divisor).astype(BF16), cont[:, size:], preferred_element_type=F32)
    for h in range(heads):
        out[:, h * size : (h + 1) * size] = result[h * rows : (h + 1) * rows].astype(BF16)


def attend(place, lengths, mine, other, cosine, sine, gain, pairs, prompt_rows):
    rows, width = mine.shape
    args = (mine, other, cosine, sine, gain, *pairs)
    out = shape_of((rows, width), BF16)
    keys = len(pairs) * pairs[0].shape[0]
    return call(
        functools.partial(attend_kernel, len(pairs), prompt_rows),
        place,
        (1,),
        [pl.BlockSpec(memory_space=pltpu.SMEM)] + [whole(a) for a in args],
        whole(out),
        out,
        (lengths, *args),
        (4 * rows * width * keys, 10 * rows * width + 512 * keys),
    )


def out_kernel(place, *refs):
    heads, weight, out = refs[:-2], refs[-2], refs[-1]
    rows = heads[0].shape[0]
    left = jnp.concatenate([head[...] for head in heads], axis=0)
    part = jnp.dot(left, weight[...], preferred_element_type=F32).astype(BF16)
    for d in range(len(heads)):
        out[place[SP] ^ d] = part[d * rows : (d + 1) * rows]


def out_parts(place, heads, weight):
    rows, depth = heads[0].shape
    width = weight.shape[1]
    step = 256 if width % 256 == 0 else width
    count = len(heads)
    return call(
        out_kernel,
        place,
        (width // step,),
        [whole(h) for h in heads] + [pl.BlockSpec((depth, step), lambda i, place: (0, i))],
        pl.BlockSpec((count, rows, step), lambda i, place: (0, 0, i)),
        shape_of((count, rows, width), BF16),
        (*heads, weight),
        (2 * count * rows * depth * width, 2 * depth * width),
    )


def final_kernel(place, parts, hidden, out):
    total = hidden[...].astype(F32)
    for t in range(parts.shape[0]):
        total = total + parts[t].astype(F32)
    out[...] = total.astype(BF16)


def final_sum(place, parts, hidden):
    count, rows, width = parts.shape
    return call(
        final_kernel,
        place,
        (1,),
        [whole(parts), whole(hidden)],
        pl.BlockSpec((rows, width), lambda i, place: (0, 0)),
        shape_of((rows, width), BF16),
        (parts, hidden),
        (count * rows * width, 12 * rows * width),
    )


def swap(array, axis, bits):
    return lax.ppermute(array, axis, [(i, i ^ bits) for i in range(lax.axis_size(axis))])


def swap_bits(count):
    bits = []
    bit = 1
    while bit < count:
        bits.append(bit)
        bit *= 2
    return bits


def gather_blocks(block, axis, count):
    held = {0: block}
    bits = swap_bits(count)
    for bit in bits[1:] + bits[:1]:
        held.update({d ^ bit: swap(held[d], axis, bit) for d in sorted(held)})
    return [held[d] for d in range(count)]


def gather_halves(first, second, axis, count):
    bits = swap_bits(count)
    firsts = {0: first}
    for bit in bits[1:]:
        firsts.update({d ^ bit: swap(firsts[d], axis, bit) for d in sorted(firsts)})
    seconds = {d: second if d == 0 else swap(firsts[d], "groups", 1) for d in firsts}
    pieces = []
    for held in (firsts, seconds):
        held.update({d ^ 1: swap(held[d], axis, 1) for d in sorted(held)})
    for d in range(count):
        pieces += [firsts[d], seconds[d]]
    return pieces


def sum_blocks(blocks, axis, count):
    held = dict(enumerate(blocks))
    bits = swap_bits(count)
    for bit in bits:
        sent = [d for d in sorted(held) if d & bit]
        got = {d ^ bit: swap(held[d], axis, bit) for d in sent}
        if bit == bits[-1]:
            return held[0], got[0]
        held = {d: held[d] + got[d] for d in got}


def tables(positions, size):
    half = size // 2
    frequency = jnp.exp(jnp.arange(half, dtype=F32) * (-2.0 * math.log(1000000.0) / size))
    angles = positions.astype(F32)[:, None] * frequency[None, :]
    cosine = jnp.cos(angles)
    sine = jnp.sin(angles)
    return (
        jnp.concatenate([cosine, cosine], axis=1),
        jnp.concatenate([-sine, sine], axis=1),
    )


def on_device(
    hidden_cont,
    hidden_prompt,
    norm_gain,
    query_weight,
    keyval_weight,
    out_weight,
    query_gain,
    key_gain,
    sample_lengths,
):
    size = query_gain.shape[0]
    heads_here = query_weight.shape[1] // size
    cont_rows = hidden_cont.shape[0]
    prompt_rows = hidden_prompt.shape[0]
    sp_index = lax.axis_index("sp")
    sp_count = lax.axis_size("sp")
    tp_index = lax.axis_index("tp")
    assert lax.axis_size("tp") == sp_count and lax.axis_size("groups") == 2
    place = jnp.stack(
        [
            sp_index,
            tp_index,
            lax.axis_index("groups"),
            tp_index * heads_here // (QH // KVH),
        ]
    ).astype(jnp.int32)
    norm_gain = norm_gain[None, :]
    query_gain = query_gain[None, :]
    key_gain = key_gain[None, :]

    cont = norm_split(place, hidden_cont, norm_gain, sp_count)
    first, second = pick_columns(place, keyval_weight, size)
    cont_all = lax.all_to_all(cont, "sp", 0, 0, tiled=True)
    weights = gather_halves(first, second, "sp", sp_count)
    prompt = norm_split(place, hidden_prompt, norm_gain, sp_count)

    index = sp_index * cont_rows + jnp.arange(cont_rows, dtype=jnp.int32)
    starts = jnp.cumsum(sample_lengths, dtype=jnp.int32) - sample_lengths
    start = jnp.max(jnp.where(index[:, None] >= starts[None, :], starts[None, :], 0), axis=1)
    prompt_pos = sp_index * prompt_rows + jnp.arange(prompt_rows, dtype=jnp.int32)
    positions = jnp.concatenate([prompt_pos, prompt_rows * sp_count + index - start])
    cosine, sine = tables(positions, size)

    parts = query_parts(place, cont_all, query_weight)
    mine, other = sum_blocks(parts, "sp", sp_count)
    pair = keyval_rows(place, prompt, cont, cosine, sine, key_gain, weights)
    pairs = gather_blocks(pair, "sp", sp_count)
    heads = attend(
        place,
        sample_lengths,
        mine,
        other,
        cosine[prompt_rows:],
        sine[prompt_rows:],
        query_gain,
        pairs,
        prompt_rows,
    )
    parts = out_parts(place, gather_blocks(heads, "sp", sp_count), out_weight)
    parts = lax.all_to_all(parts, "sp", 0, 0, tiled=True)
    parts = lax.all_to_all(parts, "tp", 0, 0, tiled=True)
    width = parts.shape[2]
    hidden = lax.dynamic_slice_in_dim(hidden_cont, tp_index * width, width, 1)
    return final_sum(place, parts, hidden)


def solution(mesh):
    placed = (
        P(("groups", "sp"), None),
        P(("groups", "sp"), None),
        P(),
        P("sp", "tp"),
        P("sp", None),
        P("tp", "sp"),
        P(),
        P(),
        P("groups"),
    )
    return jax.shard_map(
        on_device, mesh=mesh, in_specs=placed, out_specs=P(("groups", "sp"), "tp"), check_vma=False
    )
```

time: 219 us -> 88.1 us (0.40)
  waiting for transfers between devices: 159 us -> 31.1 us
  starting transfers between devices: 0.12 us -> 20.9 us
  Pallas kernels: 0 us -> 17.7 us
  matrix products: 17.4 us -> 0 us
  between operations: 13.4 us -> 0.19 us
  other arithmetic: 9.49 us -> 1.08 us
    all_gather x3 -> x0, waiting for transfers between devices: 138 us -> none  [the longest x1 62 us: on_device(): lax.all_gather(out_weight, 'sp', axis=1, tiled=True)]
    all_to_all x0 -> x2, waiting for transfers between devices: none -> 23.1 us  [the longest x1 15.9 us: on_device(): parts = lax.all_to_all(parts, 'tp', 0, 0, tiled=True)]
    reduce_scatter x1 -> x0, waiting for transfers between devices: 19.6 us -> none  [on_device(): lax.psum_scatter(partial_out.astype(jnp.bfloat16), 'tp', scatter_dimensio...]
    pallas_call x0 -> x8, Pallas kernels: none -> 17.7 us  [call(): pl.pallas_call(kernel, out_shape=out_shape, grid_spec=pltpu.PrefetchScala...]
    dot_general x5 -> x0, matrix products: 17.4 us -> none  [the longest x2 8.72 us: add_rows(): return jnp.dot(left, piece, preferred_element_type=jnp.float32)]
    all_to_all x0 -> x1, blocking collectives: none -> 12.7 us  [on_device(): parts = lax.all_to_all(parts, 'sp', 0, 0, tiled=True)]
    ppermute x0 -> x15, starting transfers between devices: none -> 12.4 us  [swap(): lax.ppermute(array, axis, [(i, i ^ bits) for i in range(lax.axis_size(axi...]
    all_gather x2 -> x0, blocking collectives: 12.2 us -> none  [the longest x1 6.72 us: on_device(): lax.all_gather(local_pairs[:prompt_rows], 'sp', axis=0, tiled=True)]
  transfers between devices with their start and end apart: 4 -> 17, of which waited for: 4 -> 8; matrix products, arithmetic and copies ran while one was open for 9% -> 2% of each run, Pallas kernels for 0% -> 11%
where the time goes in v2:
time: 88.1 us; the launch traced here: 86.4 us
  waiting for transfers between devices  31.1 us (35%)
  starting transfers between devices  20.9 us (24%)
  Pallas kernels  17.7 us (20%)
  blocking collectives  12.7 us (14%)
  local copies, waits for them, and re-layouts  2.7 us (3%)
  other arithmetic  1.08 us (1%)
    pallas_call x8, Pallas kernels, call(): pl.pallas_call(kernel, out_shape=out_shape, grid_spec=pltpu.PrefetchScala...  17.7 us
    all_to_all x1, waiting for transfers between devices, on_device(): parts = lax.all_to_all(parts, 'tp', 0, 0, tiled=True)  15.9 us
    all_to_all x1, blocking collectives, on_device(): parts = lax.all_to_all(parts, 'sp', 0, 0, tiled=True)  12.7 us
    ppermute x15, starting transfers between devices, swap(): lax.ppermute(array, axis, [(i, i ^ bits) for i in range(lax.axis_size(axi...  12.4 us
    ppermute x15, waiting for transfers between devices, swap(): lax.ppermute(array, axis, [(i, i ^ bits) for i in range(lax.axis_size(axi...  7.99 us
    all_to_all x1, waiting for transfers between devices, on_device(): cont_all = lax.all_to_all(cont, 'sp', 0, 0, tiled=True)  7.23 us
    all_to_all x1, starting transfers between devices, on_device(): parts = lax.all_to_all(parts, 'tp', 0, 0, tiled=True)  4.58 us
    all_to_all x1, starting transfers between devices, on_device(): cont_all = lax.all_to_all(cont, 'sp', 0, 0, tiled=True)  3.95 us
  transfers between devices with their start and end apart: 17, of which 8 were waited for; matrix products, arithmetic and copies ran while one was open for 2% of the time, Pallas kernels for 11%

profile of v2, /device:TPU:1, one launch (start us, length us, event | category | flops | bytes accessed | tf_op | source)
XLA Modules:
  0.0 86.4 jit_solution(6336164834451292460)
XLA Ops:
  0.1 1.7 %copy-done = bf16[1280,1024]{1,0:T(8,128)(2,1)S(1)} copy-done((bf16[1280,1024]{1,0:T(8,128)(2,1)S(1)}, bf16[1280,1024]{1,0:T(8,128)(2,1)}, u32[]{:S(2)}) %copy-start) | copy-done | bytes 2621464
  1.8 1.6 %shard_map.94 = (bf16[1280,128]{1,0:T(8,128)(2,1)}, bf16[1280,128]{1,0:T(8,128)(2,1)}) custom-call(s32[4]{0:T(128)S(1)} %pad_add_fusion.place, bf16[1280,1024]{1,0:T(8,128)(2,1)S(1)} %copy-done, bf16[1280,1024]{1,0:T(8,128)(2,1)S(1)} %copy-done), custom_call_target="tpu_custom_call" | custom-call | bytes 1310720 | tf_op jit(solution)/shard_map/pallas_call | solution.py:21
  3.4 2.0 %collective-permute-start.5 = (bf16[1280,128]{1,0:T(8,128)(2,1)}, bf16[1280,128]{1,0:T(8,128)(2,1)}, u32[]{:S(2)}, u32[]{:S(2)}) collective-permute-start(bf16[1280,128]{1,0:T(8,128)(2,1)} %get-tuple-element.15.refs_0_), channel_id=1, source_target_pairs={{0,2},{1,3},{2,0},{3,1},{4,6},{5,7},{6,4},{7,5},{8,10},{9,11},{10,... | collective-permute-start | bytes 983048 | tf_op jit(solution)/shard_map/ppermute | solution.py:279
  5.5 1.0 %collective-permute-start.3 = (bf16[1280,128]{1,0:T(8,128)(2,1)}, bf16[1280,128]{1,0:T(8,128)(2,1)}, u32[]{:S(2)}, u32[]{:S(2)}) collective-permute-start(bf16[1280,128]{1,0:T(8,128)(2,1)} %get-tuple-element.15.refs_0_), channel_id=1, source_target_pairs={{0,1},{1,0},{2,3},{3,2},{4,5},{5,4},{6,7},{7,6},{8,9},{9,8},{10,11... | collective-permute-start | bytes 983048 | tf_op jit(solution)/shard_map/ppermute | solution.py:279
  6.4 1.8 %shard_map.91.cont = bf16[4,64,1280]{2,1,0:T(8,128)(2,1)} custom-call(s32[4]{0:T(128)S(1)} %pad_add_fusion.place, bf16[64,5120]{1,0:T(8,128)(2,1)S(1)} %copy-done.4, f32[1,5120]{1,0:T(1,128)S(1)} %bitcast.10), custom_call_target="tpu_custom_call" | custom-call | flops 1310720 | bytes 1310720 | tf_op jit(solution)/shard_map/pallas_call | solution.py:21
  8.2 4.0 %all-to-all-start = ((bf16[4,64,1280]{2,1,0:T(8,128)(2,1)}), bf16[4,64,1280]{2,1,0:T(8,128)(2,1)S(1)}, u32[]{:S(2)}, u32[]{:S(2)}) async-start(bf16[4,64,1280]{2,1,0:T(8,128)(2,1)} %shard_map.91.cont), calls=%async_computation | async-start | bytes 1310720 | tf_op jit(solution)/shard_map/all_to_all | solution.py:369
  13.2 1.2 %collective-permute-start.6 = (bf16[1280,128]{1,0:T(8,128)(2,1)}, bf16[1280,128]{1,0:T(8,128)(2,1)}, u32[]{:S(2)}, u32[]{:S(2)}) collective-permute-start(bf16[1280,128]{1,0:T(8,128)(2,1)} %collective-permute-done.5.refs_4_), channel_id=1, source_target_pairs={{0,16},{16,0},{1,17},{17,1},{2,18},{18,2},{3,19},{19,3},{4,20},{20... | collective-permute-start | bytes 983048 | tf_op jit(solution)/shard_map/ppermute | solution.py:279
  14.4 7.2 %all-to-all-done.rows = bf16[4,64,1280]{2,1,0:T(8,128)(2,1)S(1)} async-done(((bf16[4,64,1280]{2,1,0:T(8,128)(2,1)}), bf16[4,64,1280]{2,1,0:T(8,128)(2,1)S(1)}, u32[]{:S(2)}, u32[]{:S(2)}) %all-to-all-start) | async-done | bytes 655392 | tf_op jit(solution)/shard_map/all_to_all | solution.py:369
  21.7 2.4 %shard_map.92 = (f32[64,1024]{1,0:T(8,128)S(1)}, f32[64,1024]{1,0:T(8,128)S(1)}, f32[64,1024]{1,0:T(8,128)S(1)}, f32[64,1024]{1,0:T(8,128)S(1)}) custom-call(s32[4]{0:T(128)S(1)} %pad_add_fusion.place, bf16[4,64,1280]{2,1,0:T(8,128)(2,1)S(1)} %all-to-all-done.rows, bf16[1280,1024]{1,0:T(8,128)(2,1)S(1)} %copy-done.1), custom_call_target="tpu_custom_call" | custom-call | flops 671088640 | bytes 2621440 | tf_op jit(solution)/shard_map/pallas_call | solution.py:21
  27.1 1.4 %shard_map.93.prompt = bf16[4,128,1280]{2,1,0:T(8,128)(2,1)S(1)} custom-call(s32[4]{0:T(128)S(1)} %pad_add_fusion.place, bf16[128,5120]{1,0:T(8,128)(2,1)S(1)} %copy-done.3, f32[1,5120]{1,0:T(1,128)S(1)} %bitcast.11), custom_call_target="tpu_custom_call" | custom-call | flops 2621440 | bytes 2621440 | tf_op jit(solution)/shard_map/pallas_call | solution.py:21
  28.6 3.8 %shard_map.95.refs_0_ = bf16[192,256]{1,0:T(8,128)(2,1)S(1)} custom-call(s32[4]{0:T(128)S(1)} %pad_add_fusion.place, bf16[4,128,1280]{2,1,0:T(8,128)(2,1)S(1)} %shard_map.93.prompt, bf16[4,64,1280]{2,1,0:T(8,128)(2,1)} %shard_map.91.cont, f32[192,128]{1,0:T(8,128)S(1)} %get-tuple-element.20.cosine, f32[192,128]{1,0:T(8,128)S(1)} %get-tuple-element.21.sine, ...), custom_call_target="tpu_custom_call" | custom-call | flops 503316480 | bytes 4587520 | tf_op jit(solution)/shard_map/pallas_call | solution.py:21
  32.4 1.1 %collective-permute-start.10 = (bf16[192,256]{1,0:T(8,128)(2,1)S(1)}, bf16[192,256]{1,0:T(8,128)(2,1)S(1)}, u32[]{:S(2)}, u32[]{:S(2)}) collective-permute-start(bf16[192,256]{1,0:T(8,128)(2,1)S(1)} %shard_map.95.refs_0_), channel_id=1, source_target_pairs={{0,2},{1,3},{2,0},{3,1},{4,6},{5,7},{6,4},{7,5},{8,10},{9,11},{10,... | collective-permute-start | bytes 294920 | tf_op jit(solution)/shard_map/ppermute | solution.py:279
  34.3 2.2 %collective-permute-done.10.refs_2_ = bf16[192,256]{1,0:T(8,128)(2,1)S(1)} collective-permute-done((bf16[192,256]{1,0:T(8,128)(2,1)S(1)}, bf16[192,256]{1,0:T(8,128)(2,1)S(1)}, u32[]{:S(2)}, u32[]{:S(2)}) %collective-permute-start.10) | collective-permute-done | bytes 98336 | tf_op jit(solution)/shard_map/ppermute | solution.py:279
  36.4 1.3 %collective-permute-start.11 = (bf16[192,256]{1,0:T(8,128)(2,1)S(1)}, bf16[192,256]{1,0:T(8,128)(2,1)S(1)}, u32[]{:S(2)}, u32[]{:S(2)}) collective-permute-start(bf16[192,256]{1,0:T(8,128)(2,1)S(1)} %collective-permute-done.10.refs_2_), channel_id=1, source_target_pairs={{0,1},{1,0},{2,3},{3,2},{4,5},{5,4},{6,7},{7,6},{8,9},{9,8},{10,11... | collective-permute-start | bytes 294920 | tf_op jit(solution)/shard_map/ppermute | solution.py:279
  38.7 3.0 %shard_map.96.refs_0_ = bf16[64,1024]{1,0:T(8,128)(2,1)S(1)} custom-call(s32[4]{0:T(128)S(1)} %pad_add_fusion.place, s32[8]{0:T(128)S(1)} %copy-done.6, f32[64,1024]{1,0:T(8,128)S(1)} %add.38.mine, f32[64,1024]{1,0:T(8,128)S(1)} %collective-permute-done.2.other, f32[64,128]{1,0:T(8,128)S(1)} %get-tuple-element.23.cosine, ...), custom_call_target="tpu_custom_call" | custom-call | flops 201326592 | bytes 1048576 | tf_op jit(solution)/shard_map/pallas_call | solution.py:21
  41.6 1.1 %collective-permute-start.13 = (bf16[64,1024]{1,0:T(8,128)(2,1)S(1)}, bf16[64,1024]{1,0:T(8,128)(2,1)S(1)}, u32[]{:S(2)}, u32[]{:S(2)}) collective-permute-start(bf16[64,1024]{1,0:T(8,128)(2,1)S(1)} %shard_map.96.refs_0_), channel_id=1, source_target_pairs={{0,2},{1,3},{2,0},{3,1},{4,6},{5,7},{6,4},{7,5},{8,10},{9,11},{10,... | collective-permute-start | bytes 393224 | tf_op jit(solution)/shard_map/ppermute | solution.py:279
  43.4 3.0 %collective-permute-done.13.refs_2_ = bf16[64,1024]{1,0:T(8,128)(2,1)S(1)} collective-permute-done((bf16[64,1024]{1,0:T(8,128)(2,1)S(1)}, bf16[64,1024]{1,0:T(8,128)(2,1)S(1)}, u32[]{:S(2)}, u32[]{:S(2)}) %collective-permute-start.13) | collective-permute-done | bytes 131104 | tf_op jit(solution)/shard_map/ppermute | solution.py:279
  46.4 1.2 %collective-permute-start.14 = (bf16[64,1024]{1,0:T(8,128)(2,1)S(1)}, bf16[64,1024]{1,0:T(8,128)(2,1)S(1)}, u32[]{:S(2)}, u32[]{:S(2)}) collective-permute-start(bf16[64,1024]{1,0:T(8,128)(2,1)S(1)} %collective-permute-done.13.refs_2_), channel_id=1, source_target_pairs={{0,1},{1,0},{2,3},{3,2},{4,5},{5,4},{6,7},{7,6},{8,9},{9,8},{10,11... | collective-permute-start | bytes 393224 | tf_op jit(solution)/shard_map/ppermute | solution.py:279
  47.6 1.0 %collective-permute-done.14.refs_3_ = bf16[64,1024]{1,0:T(8,128)(2,1)S(1)} collective-permute-done((bf16[64,1024]{1,0:T(8,128)(2,1)S(1)}, bf16[64,1024]{1,0:T(8,128)(2,1)S(1)}, u32[]{:S(2)}, u32[]{:S(2)}) %collective-permute-start.14) | collective-permute-done | bytes 131104 | tf_op jit(solution)/shard_map/ppermute | solution.py:279
  48.6 2.4 %shard_map.97 = bf16[4,64,1280]{2,1,0:T(8,128)(2,1)S(1)} custom-call(s32[4]{0:T(128)S(1)} %pad_add_fusion.place, bf16[64,1024]{1,0:T(8,128)(2,1)S(1)} %shard_map.96.refs_0_, bf16[64,1024]{1,0:T(8,128)(2,1)S(1)} %collective-permute-done.12.refs_1_, bf16[64,1024]{1,0:T(8,128)(2,1)S(1)} %collective-permute-done.13.refs_2_, ...), custom_call_target="tpu_custom_call" | custom-call | flops 671088640 | bytes 2621440 | tf_op jit(solution)/shard_map/pallas_call | solution.py:21
  51.0 12.7 %all_to_all.15 = bf16[4,64,1280]{2,1,0:T(8,128)(2,1)} all-to-all(bf16[4,64,1280]{2,1,0:T(8,128)(2,1)S(1)} %shard_map.97), channel_id=1, replica_groups=mesh['groups'=2,'tp'=4,'sp'=4] {'sp'}, dimensions={0} | all-to-all | bytes 1310720 | tf_op jit(solution)/shard_map/all_to_all | solution.py:396
  63.7 4.6 %all-to-all-start.2 = ((bf16[4,64,1280]{2,1,0:T(8,128)(2,1)}), bf16[4,64,1280]{2,1,0:T(8,128)(2,1)S(1)}, u32[]{:S(2)}, u32[]{:S(2)}) async-start(bf16[4,64,1280]{2,1,0:T(8,128)(2,1)} %all_to_all.15), calls=%async_computation.2 | async-start | bytes 1310720 | tf_op jit(solution)/shard_map/all_to_all | solution.py:397
  69.2 15.9 %all-to-all-done.2.parts = bf16[4,64,1280]{2,1,0:T(8,128)(2,1)S(1)} async-done(((bf16[4,64,1280]{2,1,0:T(8,128)(2,1)}), bf16[4,64,1280]{2,1,0:T(8,128)(2,1)S(1)}, u32[]{:S(2)}, u32[]{:S(2)}) %all-to-all-start.2) | async-done | bytes 655392 | tf_op jit(solution)/shard_map/all_to_all | solution.py:397
  85.0 1.3 %shard_map.98 = bf16[64,1280]{1,0:T(8,128)(2,1)} custom-call(s32[4]{0:T(128)S(1)} %pad_add_fusion.place, bf16[4,64,1280]{2,1,0:T(8,128)(2,1)S(1)} %all-to-all-done.2.parts, bf16[64,1280]{1,0:T(8,128)(2,1)S(1)} %constant_dynamic-slice_fusion.hidden), custom_call_target="tpu_custom_call" | custom-call | flops 327680 | bytes 983040 | tf_op jit(solution)/shard_map/pallas_call | solution.py:21
  (52 shorter events, 7.4 us)
Async XLA Ops:
  1.8 4.6 %copy-start.4 = (bf16[64,5120]{1,0:T(8,128)(2,1)S(1)}, bf16[64,5120]{1,0:T(8,128)(2,1)}, u32[]{:S(2)}) copy-start(bf16[64,5120]{1,0:T(8,128)(2,1)} %hidden.2) | copy-start | bytes 1966084
  1.8 4.6 %copy-start.5 = (f32[5120]{0:T(1024)S(1)}, f32[5120]{0:T(1024)}, u32[]{:S(2)}) copy-start(f32[5120]{0:T(1024)} %param.11) | copy-start | bytes 61444
  3.4 8.7 %copy-start.6 = (s32[8]{0:T(128)S(1)}, s32[8]{0:T(128)}, u32[]{:S(2)}) copy-start(s32[8]{0:T(128)} %lengths.1) | copy-start | bytes 100
  3.4 18.2 %copy-start.1 = (bf16[1280,1024]{1,0:T(8,128)(2,1)S(1)}, bf16[1280,1024]{1,0:T(8,128)(2,1)}, u32[]{:S(2)}) copy-start(bf16[1280,1024]{1,0:T(8,128)(2,1)} %weight.1) | copy-start | bytes 7864324
  3.4 9.8 %collective-permute-start.5 = (bf16[1280,128]{1,0:T(8,128)(2,1)}, bf16[1280,128]{1,0:T(8,128)(2,1)}, u32[]{:S(2)}, u32[]{:S(2)}) collective-permute-start(bf16[1280,128]{1,0:T(8,128)(2,1)} %get-tuple-element.15.refs_0_), channel_id=1, source_target_pairs={{0,2},{1,3},{2,0},{3,1},{4,6},{5,7},{6,4},{7,5},{8,10},{9,11},{10,... | collective-permute-start | bytes 983048 | tf_op jit(solution)/shard_map/ppermute | solution.py:279
  5.5 21.0 %collective-permute-start.3 = (bf16[1280,128]{1,0:T(8,128)(2,1)}, bf16[1280,128]{1,0:T(8,128)(2,1)}, u32[]{:S(2)}, u32[]{:S(2)}) collective-permute-start(bf16[1280,128]{1,0:T(8,128)(2,1)} %get-tuple-element.15.refs_0_), channel_id=1, source_target_pairs={{0,1},{1,0},{2,3},{3,2},{4,5},{5,4},{6,7},{7,6},{8,9},{9,8},{10,11... | collective-permute-start | bytes 983048 | tf_op jit(solution)/shard_map/ppermute | solution.py:279
  6.4 22.1 %collective-permute-start.4 = (bf16[1280,128]{1,0:T(8,128)(2,1)}, bf16[1280,128]{1,0:T(8,128)(2,1)}, u32[]{:S(2)}, u32[]{:S(2)}) collective-permute-start(bf16[1280,128]{1,0:T(8,128)(2,1)} %get-tuple-element.16.refs_1_), channel_id=1, source_target_pairs={{0,1},{1,0},{2,3},{3,2},{4,5},{5,4},{6,7},{7,6},{8,9},{9,8},{10,11... | collective-permute-start | bytes 983048 | tf_op jit(solution)/shard_map/ppermute | solution.py:279
  8.2 13.4 %all-to-all-start = ((bf16[4,64,1280]{2,1,0:T(8,128)(2,1)}), bf16[4,64,1280]{2,1,0:T(8,128)(2,1)S(1)}, u32[]{:S(2)}, u32[]{:S(2)}) async-start(bf16[4,64,1280]{2,1,0:T(8,128)(2,1)} %shard_map.91.cont), calls=%async_computation | async-start | bytes 1310720 | tf_op jit(solution)/shard_map/all_to_all | solution.py:369
  13.2 11.8 %collective-permute-start.6 = (bf16[1280,128]{1,0:T(8,128)(2,1)}, bf16[1280,128]{1,0:T(8,128)(2,1)}, u32[]{:S(2)}, u32[]{:S(2)}) collective-permute-start(bf16[1280,128]{1,0:T(8,128)(2,1)} %collective-permute-done.5.refs_4_), channel_id=1, source_target_pairs={{0,16},{16,0},{1,17},{17,1},{2,18},{18,2},{3,19},{19,3},{4,20},{20... | collective-permute-start | bytes 983048 | tf_op jit(solution)/shard_map/ppermute | solution.py:279
  21.6 5.5 %copy-start.3 = (bf16[128,5120]{1,0:T(8,128)(2,1)S(1)}, bf16[128,5120]{1,0:T(8,128)(2,1)}, u32[]{:S(2)}) copy-start(bf16[128,5120]{1,0:T(8,128)(2,1)} %hidden.3) | copy-start | bytes 3932164
  24.1 2.0 %collective-permute-start.1 = (f32[64,1024]{1,0:T(8,128)S(1)}, f32[64,1024]{1,0:T(8,128)S(1)}, u32[]{:S(2)}, u32[]{:S(2)}) collective-permute-start(f32[64,1024]{1,0:T(8,128)S(1)} %get-tuple-element.14), channel_id=1, source_target_pairs={{0,1},{1,0},{2,3},{3,2},{4,5},{5,4},{6,7},{7,6},{8,9},{9,8},{10,11... | collective-permute-start | bytes 786440 | tf_op jit(solution)/shard_map/ppermute | solution.py:279
  24.9 3.6 %collective-permute-start.7 = (bf16[1280,128]{1,0:T(8,128)(2,1)}, bf16[1280,128]{1,0:T(8,128)(2,1)S(1)}, u32[]{:S(2)}, u32[]{:S(2)}) collective-permute-start(bf16[1280,128]{1,0:T(8,128)(2,1)} %collective-permute-done.5.refs_4_), channel_id=1, source_target_pairs={{0,1},{1,0},{2,3},{3,2},{4,5},{5,4},{6,7},{7,6},{8,9},{9,8},{10,11... | collective-permute-start | bytes 983048 | tf_op jit(solution)/shard_map/ppermute | solution.py:279
  25.0 3.6 %collective-permute-start.8 = (bf16[1280,128]{1,0:T(8,128)(2,1)}, bf16[1280,128]{1,0:T(8,128)(2,1)S(1)}, u32[]{:S(2)}, u32[]{:S(2)}) collective-permute-start(bf16[1280,128]{1,0:T(8,128)(2,1)} %collective-permute-done.6.refs_5_), channel_id=1, source_target_pairs={{0,1},{1,0},{2,3},{3,2},{4,5},{5,4},{6,7},{7,6},{8,9},{9,8},{10,11... | collective-permute-start | bytes 983048 | tf_op jit(solution)/shard_map/ppermute | solution.py:279
  26.1 11.7 %collective-permute-start = (f32[64,1024]{1,0:T(8,128)S(1)}, f32[64,1024]{1,0:T(8,128)S(1)}, u32[]{:S(2)}, u32[]{:S(2)}) collective-permute-start(f32[64,1024]{1,0:T(8,128)S(1)} %get-tuple-element.12), channel_id=1, source_target_pairs={{0,1},{1,0},{2,3},{3,2},{4,5},{5,4},{6,7},{7,6},{8,9},{9,8},{10,11... | collective-permute-start | bytes 786440 | tf_op jit(solution)/shard_map/ppermute | solution.py:279
  26.5 11.4 %collective-permute-start.2 = (f32[64,1024]{1,0:T(8,128)S(1)}, f32[64,1024]{1,0:T(8,128)S(1)}, u32[]{:S(2)}, u32[]{:S(2)}) collective-permute-start(f32[64,1024]{1,0:T(8,128)S(1)} %add.39), channel_id=1, source_target_pairs={{0,2},{1,3},{2,0},{3,1},{4,6},{5,7},{6,4},{7,5},{8,10},{9,11},{10,... | collective-permute-start | bytes 786440 | tf_op jit(solution)/shard_map/ppermute | solution.py:279
  28.6 10.1 %copy-start.7 = (f32[128]{0:T(128)S(1)}, f32[128]{0:T(128)}, u32[]{:S(2)}) copy-start(f32[128]{0:T(128)} %param.15) | copy-start | bytes 1540
  28.6 20.0 %copy-start.2 = (bf16[1024,1280]{1,0:T(8,128)(2,1)S(1)}, bf16[1024,1280]{1,0:T(8,128)(2,1)}, u32[]{:S(2)}) copy-start(bf16[1024,1280]{1,0:T(8,128)(2,1)} %refs_4_.1) | copy-start | bytes 7864324
  32.4 4.0 %collective-permute-start.10 = (bf16[192,256]{1,0:T(8,128)(2,1)S(1)}, bf16[192,256]{1,0:T(8,128)(2,1)S(1)}, u32[]{:S(2)}, u32[]{:S(2)}) collective-permute-start(bf16[192,256]{1,0:T(8,128)(2,1)S(1)} %shard_map.95.refs_0_), channel_id=1, source_target_pairs={{0,2},{1,3},{2,0},{3,1},{4,6},{5,7},{6,4},{7,5},{8,10},{9,11},{10,... | collective-permute-start | bytes 294920 | tf_op jit(solution)/shard_map/ppermute | solution.py:279
  33.6 4.3 %collective-permute-start.9 = (bf16[192,256]{1,0:T(8,128)(2,1)S(1)}, bf16[192,256]{1,0:T(8,128)(2,1)S(1)}, u32[]{:S(2)}, u32[]{:S(2)}) collective-permute-start(bf16[192,256]{1,0:T(8,128)(2,1)S(1)} %shard_map.95.refs_0_), channel_id=1, source_target_pairs={{0,1},{1,0},{2,3},{3,2},{4,5},{5,4},{6,7},{7,6},{8,9},{9,8},{10,11... | collective-permute-start | bytes 294920 | tf_op jit(solution)/shard_map/ppermute | solution.py:279
  36.4 2.2 %collective-permute-start.11 = (bf16[192,256]{1,0:T(8,128)(2,1)S(1)}, bf16[192,256]{1,0:T(8,128)(2,1)S(1)}, u32[]{:S(2)}, u32[]{:S(2)}) collective-permute-start(bf16[192,256]{1,0:T(8,128)(2,1)S(1)} %collective-permute-done.10.refs_2_), channel_id=1, source_target_pairs={{0,1},{1,0},{2,3},{3,2},{4,5},{5,4},{6,7},{7,6},{8,9},{9,8},{10,11... | collective-permute-start | bytes 294920 | tf_op jit(solution)/shard_map/ppermute | solution.py:279
  41.6 4.8 %collective-permute-start.13 = (bf16[64,1024]{1,0:T(8,128)(2,1)S(1)}, bf16[64,1024]{1,0:T(8,128)(2,1)S(1)}, u32[]{:S(2)}, u32[]{:S(2)}) collective-permute-start(bf16[64,1024]{1,0:T(8,128)(2,1)S(1)} %shard_map.96.refs_0_), channel_id=1, source_target_pairs={{0,2},{1,3},{2,0},{3,1},{4,6},{5,7},{6,4},{7,5},{8,10},{9,11},{10,... | collective-permute-start | bytes 393224 | tf_op jit(solution)/shard_map/ppermute | solution.py:279
  42.8 4.9 %collective-permute-start.12 = (bf16[64,1024]{1,0:T(8,128)(2,1)S(1)}, bf16[64,1024]{1,0:T(8,128)(2,1)S(1)}, u32[]{:S(2)}, u32[]{:S(2)}) collective-permute-start(bf16[64,1024]{1,0:T(8,128)(2,1)S(1)} %shard_map.96.refs_0_), channel_id=1, source_target_pairs={{0,1},{1,0},{2,3},{3,2},{4,5},{5,4},{6,7},{7,6},{8,9},{9,8},{10,11... | collective-permute-start | bytes 393224 | tf_op jit(solution)/shard_map/ppermute | solution.py:279
  46.4 2.2 %collective-permute-start.14 = (bf16[64,1024]{1,0:T(8,128)(2,1)S(1)}, bf16[64,1024]{1,0:T(8,128)(2,1)S(1)}, u32[]{:S(2)}, u32[]{:S(2)}) collective-permute-start(bf16[64,1024]{1,0:T(8,128)(2,1)S(1)} %collective-permute-done.13.refs_2_), channel_id=1, source_target_pairs={{0,1},{1,0},{2,3},{3,2},{4,5},{5,4},{6,7},{7,6},{8,9},{9,8},{10,11... | collective-permute-start | bytes 393224 | tf_op jit(solution)/shard_map/ppermute | solution.py:279
  63.7 21.4 %all-to-all-start.2 = ((bf16[4,64,1280]{2,1,0:T(8,128)(2,1)}), bf16[4,64,1280]{2,1,0:T(8,128)(2,1)S(1)}, u32[]{:S(2)}, u32[]{:S(2)}) async-start(bf16[4,64,1280]{2,1,0:T(8,128)(2,1)} %all_to_all.15), calls=%async_computation.2 | async-start | bytes 1310720 | tf_op jit(solution)/shard_map/all_to_all | solution.py:397
  (2 other events, 6.2 us)
